TPU v7x, 32 devices: a whole 2x2x4 slice. The times are simulated.
32 devices in a mesh: row: 4 (over y, x), col: 4 (over z), layer: 2 (over core).
Axes of the slice: x: 2, y: 2, z: 4, core: 2. Of those that a mesh axis runs over, the one named last changes fastest.
Arguments:
- a_blocks: bfloat16 [4, 4, 2, 16, 2, 128, 128], P('row', 'col', 'layer'), may hold values from -6 to 6
- a_cols: int32 [4, 4, 2, 16, 2], P('row', 'col', 'layer'), may hold values from 0 to 47, as said below
- a_count: int32 [4, 4, 2, 16], P('row', 'col', 'layer'), may hold values from 1 to 2
- b_blocks: bfloat16 [4, 4, 2, 48, 2, 128, 128], P('row', 'col', 'layer'), may hold values from -0.5 to 0.5
- b_cols: int32 [4, 4, 2, 48, 2], P('row', 'col', 'layer'), may hold values from 0 to 47, as said below
- b_count: int32 [4, 4, 2, 48], P('row', 'col', 'layer'), may hold values from 1 to 2
- c_cols: int32 [4, 4, 16, 2], P('row', 'col'), may hold values from 0 to 47, as said below
Outputs:
- c_blocks: bfloat16 [4, 4, 16, 2, 128, 128], P('row', 'col', 'layer')
Inputs may be any that keep to these rules, and one draw needn't show every extreme that they name: a_cols of block row r is one of 3 * r - 1, 3 * r, 3 * r + 1 modulo 48; the slots of one block row are distinct. b_cols of block row m is one of m - 1, m, m + 1 modulo 48; the slots of one block row are distinct. c_cols of block row r is one of 3 * r - 1, 3 * r, 3 * r + 1 modulo 48; the slots of one block row are distinct.
All inputs are finite; a program needn't handle non-finite values.
Results may differ from a plain program's by a relative error of at most 0.001.
Values may be sent and summed in bfloat16 or wider, within the bound.
A program may use at most 64 MiB of HBM per device.

v0:
```python
import jax
import jax.numpy as jnp
from jax import lax
from jax.sharding import PartitionSpec as P

STEPS = 2


def passed_along(value, axis, steps):
    count = lax.axis_size(axis)
    pairs = [(source, (source + steps) % count) for source in range(count)]
    return lax.ppermute(value, axis, pairs)


def pick_rows(panel, index, live, wanted):
    return (
        jnp.take(panel, wanted, axis=0),
        jnp.take(index, wanted, axis=0),
        jnp.take(live, wanted, axis=0),
    )


def panel_terms(a_panel, a_live, chosen, chosen_cols, chosen_live, out_cols):
    slot_a = lax.broadcasted_iota(jnp.int32, chosen_cols.shape, 1)
    slot_b = lax.broadcasted_iota(jnp.int32, chosen_cols.shape, 2)
    usable = (slot_a < a_live[:, None, None]) & (slot_b < chosen_live[:, :, None])
    matches = (chosen_cols[:, :, :, None] == out_cols[:, None, None, :]) & usable[:, :, :, None]
    products = jnp.einsum("rtxy,rtuyz->rtuxz", a_panel, chosen, preferred_element_type=jnp.float32)
    return jnp.einsum(
        "rtuv,rtuxz->rvxz", matches.astype(jnp.float32), products, precision=lax.Precision.HIGHEST
    )


def local(a_blocks, a_cols, a_count, b_blocks, b_cols, b_count, c_cols):
    a_panel = a_blocks[0, 0, 0]
    a_index = a_cols[0, 0, 0]
    a_live = a_count[0, 0, 0]
    b_panel = b_blocks[0, 0, 0]
    b_index = b_cols[0, 0, 0]
    b_live = b_count[0, 0, 0]
    out_cols = c_cols[0, 0]
    partial_value = jnp.zeros(
        (out_cols.shape[0], out_cols.shape[1], a_panel.shape[2], b_panel.shape[3]), jnp.float32
    )
    for cannon_step in range(STEPS):
        if cannon_step > 0:
            a_panel, a_index, a_live = passed_along((a_panel, a_index, a_live), "col", -1)
        if cannon_step > 0:
            b_panel, b_index, b_live = passed_along((b_panel, b_index, b_live), "row", -1)
        chosen, chosen_cols, chosen_live = pick_rows(b_panel, b_index, b_live, a_index)
        partial_value = partial_value + panel_terms(
            a_panel, a_live, chosen, chosen_cols, chosen_live, out_cols
        )
    summed = lax.psum_scatter(partial_value, "layer", scatter_dimension=0, tiled=True)
    return summed.astype(jnp.bfloat16)[None, None]


def solution(mesh):
    return jax.shard_map(
        local,
        mesh=mesh,
        in_specs=(
            P("row", "col", "layer", None, None, None, None),
            P("row", "col", "layer", None, None),
            P("row", "col", "layer", None),
            P("row", "col", "layer", None, None, None, None),
            P("row", "col", "layer", None, None),
            P("row", "col", "layer", None),
            P("row", "col", None, None),
        ),
        out_specs=P("row", "col", "layer", None, None, None),
        check_vma=False,
    )
```

profile of v0, /device:TPU:0, one launch (start us, length us, event | category | flops | bytes accessed | tf_op | source)
XLA Modules:
  0.0 130.6 jit_solution(15482733557025326005)
XLA Ops:
  6.5 3.9 %collective-permute-start.4 = (bf16[48,2,128,128]{3,2,1,0:T(8,128)(2,1)}, bf16[48,2,128,128]{3,2,1,0:T(8,128)(2,1)}, u32[]{:S(2)}, u32[]{:S(2)}) collective-permute-start(bf16[48,2,128,128]{3,2,1,0:T(8,128)(2,1)} %bitcast.54), channel_id=1, source_target_pairs={{0,24},{8,0},{16,8},{24,16},{1,25},{9,1},{17,9},{25,17},{2,26},{10... | collective-permute-start | bytes 9437192 | tf_op jit(solution)/shard_map/ppermute | solution.py:12
  10.4 3.6 %collective-permute-start.2 = (s32[16]{0:T(128)}, s32[16]{0:T(128)S(1)}, u32[]{:S(2)}, u32[]{:S(2)}) collective-permute-start(s32[16]{0:T(128)} %bitcast.62), channel_id=1, source_target_pairs={{0,6},{2,0},{4,2},{6,4},{1,7},{3,1},{5,3},{7,5},{8,14},{10,8},{12,... | collective-permute-start | bytes 200 | tf_op jit(solution)/shard_map/ppermute | solution.py:12
  14.0 0.5 collective-permute-start.3
  14.6 0.4 collective-permute-start.1
  15.0 0.4 collective-permute-start.5
  15.5 0.7 compare_select_fusion.1
  16.4 0.7 gather_fusion.1
  17.1 2.9 %gather_fusion.2 = bf16[32,2,128,128]{3,2,1,0:T(8,128)(2,1)S(1)} fusion(bf16[48,2,128,128]{3,2,1,0:T(8,128)(2,1)} %bitcast.55, s32[1024]{0:T(1024)S(1)} %pad_clamp_fusion.1), kind=kCustom, calls=%fused_computation.2.clone | custom fusion | bytes 4194432 | tf_op jit(solution)/shard_map/jit(_take)/gather | solution.py:17
  20.1 0.1 copy.52
  20.5 0.6 gather_fusion
  21.1 0.2 copy.84
  21.3 0.2 copy.56
  21.5 2.7 %copy.63 = bf16[16,2,2,128,128]{3,4,2,1,0:T(8,128)(2,1)} copy(bf16[16,2,2,128,128]{4,3,2,1,0:T(8,128)(2,1)S(1)} %bitcast.52) | data formatting | bytes 4194304 | tf_op jit(solution)/shard_map/jit(_take)/gather | solution.py:17
  24.2 4.3 %convolution_bitcast_fusion.1 = f32[16,2,2,128,128]{3,4,2,1,0:T(8,128)} fusion(bf16[16,2,2,128,128]{3,4,2,1,0:T(8,128)(2,1)} %copy.63, pred[16,2]{1,0:T(8,128)(4,1)S(1)} %copy.52, bf16[1,1,1,16,2,128,128]{6,5,4,3,2,1,0:T(8,128)(2,1)S(1)} %copy-done.1), kind=kOutput, calls=%fused_computation.7 | convolution fusion | flops 269484032 | bytes 7340064 | tf_op jit(solution)/shard_map/rtxy,rtuyz->rtuxz/dot_general | solution.py:28
  28.5 7.2 %copy.64 = f32[16,2,2,128,128]{4,2,1,3,0:T(2,128)} copy(f32[16,2,2,128,128]{3,4,2,1,0:T(8,128)} %convolution_bitcast_fusion.1) | data formatting | bytes 8388608 | tf_op jit(solution)/shard_map/rtxy,rtuyz->rtuxz/transpose | solution.py:28
  35.7 0.1 compare_and_fusion.1
  35.8 10.7 %fusion.9 = f32[16,2,128,128,1]{3,1,4,2,0:T(2,128)} fusion(f32[16,2,2,128,128]{4,2,1,3,0:T(2,128)} %copy.64, pred[16,2,2]{2,1,0:T(4,128)(4,1)S(1)} %compare_and_fusion.1, s32[16,2]{1,0:T(8,128)S(1)} %copy.57, s32[16,2,2]{2,1,0:T(2,128)S(1)} %copy.56), kind=kOutput, calls=%fused_computation.19 | convolution fusion | flops 25166080 | bytes 6291904 | tf_op jit(solution)/shard_map/rtuv,rtuxz->rvxz/dot_general | solution.py:29
  46.5 1.4 %collective-permute-start = (s32[48,2]{1,0:T(8,128)S(1)}, s32[48,2]{1,0:T(8,128)S(1)}, u32[]{:S(2)}, u32[]{:S(2)}) collective-permute-start(s32[48,2]{1,0:T(8,128)S(1)} %copy.54), channel_id=1, source_target_pairs={{0,24},{8,0},{16,8},{24,16},{1,25},{9,1},{17,9},{25,17},{2,26},{10... | collective-permute-start | bytes 1160 | tf_op jit(solution)/shard_map/ppermute | solution.py:12
  48.2 30.2 %collective-permute-done.3 = s32[48]{0:T(128)S(1)} collective-permute-done((s32[48]{0:T(128)}, s32[48]{0:T(128)S(1)}, u32[]{:S(2)}, u32[]{:S(2)}) %collective-permute-start.3) | collective-permute-done | bytes 224 | tf_op jit(solution)/shard_map/ppermute | solution.py:12
  78.4 0.7 gather_fusion.4
  79.3 0.1 compare_and_fusion
  79.6 0.6 gather_fusion.3
  80.1 0.2 copy.85
  80.4 0.2 copy.69
  80.6 2.8 %gather_fusion.5 = bf16[32,2,128,128]{3,2,1,0:T(8,128)(2,1)S(1)} fusion(bf16[48,2,128,128]{3,2,1,0:T(8,128)(2,1)} %collective-permute-done.4, s32[1024]{0:T(1024)S(1)} %pad_clamp_fusion), kind=kCustom, calls=%fused_computation.5.clone | custom fusion | bytes 4194432 | tf_op jit(solution)/shard_map/jit(_take)/gather | solution.py:17
  83.4 2.7 %copy.75 = bf16[16,2,2,128,128]{3,4,2,1,0:T(8,128)(2,1)} copy(bf16[16,2,2,128,128]{4,3,2,1,0:T(8,128)(2,1)S(1)} %bitcast.53) | data formatting | bytes 4194304 | tf_op jit(solution)/shard_map/jit(_take)/gather | solution.py:17
  86.1 4.6 %convolution_bitcast_fusion = f32[16,2,2,128,128]{3,4,2,1,0:T(8,128)} fusion(bf16[16,2,2,128,128]{3,4,2,1,0:T(8,128)(2,1)} %copy.75, pred[16,2]{1,0:T(8,128)(4,1)S(1)} %copy.65, bf16[16,2,128,128]{3,2,1,0:T(8,128)(2,1)} %collective-permute-done.5), kind=kOutput, calls=%fused_computation.6 | convolution fusion | flops 269484032 | bytes 7340064 | tf_op jit(solution)/shard_map/rtxy,rtuyz->rtuxz/dot_general | solution.py:28
  90.7 7.4 %copy.76 = f32[16,2,2,128,128]{4,2,1,3,0:T(2,128)} copy(f32[16,2,2,128,128]{3,4,2,1,0:T(8,128)} %convolution_bitcast_fusion) | data formatting | bytes 8388608 | tf_op jit(solution)/shard_map/rtxy,rtuyz->rtuxz/transpose | solution.py:28
  98.1 10.0 %bitcast_add_fusion = f32[16,2,128,128]{3,1,2,0:T(2,128)S(1)} fusion(f32[16,2,128,128,1]{3,1,4,2,0:T(2,128)S(1)} %copy-done.6, f32[16,2,2,128,128]{4,2,1,3,0:T(2,128)} %copy.76, pred[16,2,2]{2,1,0:T(4,128)(4,1)S(1)} %compare_and_fusion, s32[16,2,2]{2,1,0:T(2,128)S(1)} %copy.69, s32[16,2]{1,0:T(8,128)S(1)} %copy.57), kind=kOutput, calls=%fused_computation.8 | convolution fusion | flops 25690368 | bytes 8389056 | tf_op jit(solution)/shard_map/rtuv,rtuxz->rvxz/dot_general | solution.py:29
  108.1 1.6 %copy.77 = f32[16,2,128,128]{3,2,1,0:T(8,128)} copy(f32[16,2,128,128]{3,1,2,0:T(2,128)S(1)} %bitcast_add_fusion) | data formatting | bytes 4194304 | tf_op jit(solution)/shard_map/add | solution.py:51
  109.7 12.0 %reduce-scatter.2.cloned.1.call-done = f32[8,2,128,128]{3,2,1,0:T(8,128)} async-done(((f32[16,2,128,128]{3,2,1,0:T(8,128)}), f32[8,2,128,128]{3,2,1,0:T(8,128)}) %reduce-scatter.2.cloned.1.call-update) | async-done | bytes 1048592 | tf_op jit(solution)/shard_map/reduce_scatter | solution.py:54
  121.7 2.1 %convert_bitcast_fusion = bf16[1,1,8,2,128,128]{5,4,3,2,1,0:T(8,128)(2,1)} fusion(f32[8,2,128,128]{3,2,1,0:T(8,128)} %reduce-scatter.2.cloned.1.call-done), kind=kLoop, calls=%fused_computation.17 | loop fusion | flops 262144 | bytes 1572864 | tf_op jit(solution)/shard_map/broadcast_in_dim | solution.py:55
  (41 shorter events, 1.2 us)
Async XLA Ops:
  6.5 9.8 %copy-start = (s32[1,1,1,48]{3,2,1,0:T(1,128)S(1)}, s32[1,1,1,48]{3,2,1,0:T(1,128)}, u32[]{:S(2)}) copy-start(s32[1,1,1,48]{3,2,1,0:T(1,128)} %param.18) | copy-start | bytes 580
  6.5 115.2 %reduce-scatter.2.cloned.1.call-start = ((), (), s32[]{:S(2)}) async-start(), calls=%async_computation.1 | async-start | bytes 3145728 | tf_op jit(solution)/shard_map/reduce_scatter | solution.py:54
  6.5 74.0 %collective-permute-start.4 = (bf16[48,2,128,128]{3,2,1,0:T(8,128)(2,1)}, bf16[48,2,128,128]{3,2,1,0:T(8,128)(2,1)}, u32[]{:S(2)}, u32[]{:S(2)}) collective-permute-start(bf16[48,2,128,128]{3,2,1,0:T(8,128)(2,1)} %bitcast.54), channel_id=1, source_target_pairs={{0,24},{8,0},{16,8},{24,16},{1,25},{9,1},{17,9},{25,17},{2,26},{10... | collective-permute-start | bytes 9437192 | tf_op jit(solution)/shard_map/ppermute | solution.py:12
  10.4 68.9 %collective-permute-start.2 = (s32[16]{0:T(128)}, s32[16]{0:T(128)S(1)}, u32[]{:S(2)}, u32[]{:S(2)}) collective-permute-start(s32[16]{0:T(128)} %bitcast.62), channel_id=1, source_target_pairs={{0,6},{2,0},{4,2},{6,4},{1,7},{3,1},{5,3},{7,5},{8,14},{10,8},{12,... | collective-permute-start | bytes 200 | tf_op jit(solution)/shard_map/ppermute | solution.py:12
  14.0 64.3 %collective-permute-start.3 = (s32[48]{0:T(128)}, s32[48]{0:T(128)S(1)}, u32[]{:S(2)}, u32[]{:S(2)}) collective-permute-start(s32[48]{0:T(128)} %bitcast.50), channel_id=1, source_target_pairs={{0,24},{8,0},{16,8},{24,16},{1,25},{9,1},{17,9},{25,17},{2,26},{10... | collective-permute-start | bytes 584 | tf_op jit(solution)/shard_map/ppermute | solution.py:12
  14.6 32.0 %collective-permute-start.1 = (s32[16,2]{0,1:T(2,128)}, s32[16,2]{0,1:T(2,128)S(1)}, u32[]{:S(2)}, u32[]{:S(2)}) collective-permute-start(s32[16,2]{0,1:T(2,128)} %bitcast.59), channel_id=1, source_target_pairs={{0,6},{2,0},{4,2},{6,4},{1,7},{3,1},{5,3},{7,5},{8,14},{10,8},{12,... | collective-permute-start | bytes 392 | tf_op jit(solution)/shard_map/ppermute | solution.py:12
  15.0 71.1 %collective-permute-start.5 = (bf16[16,2,128,128]{3,2,1,0:T(8,128)(2,1)}, bf16[16,2,128,128]{3,2,1,0:T(8,128)(2,1)}, u32[]{:S(2)}, u32[]{:S(2)}) collective-permute-start(bf16[16,2,128,128]{3,2,1,0:T(8,128)(2,1)} %bitcast.56), channel_id=1, source_target_pairs={{0,6},{2,0},{4,2},{6,4},{1,7},{3,1},{5,3},{7,5},{8,14},{10,8},{12,... | collective-permute-start | bytes 3145736 | tf_op jit(solution)/shard_map/ppermute | solution.py:12
  17.1 3.1 %copy-start.2 = (s32[1,1,1,16,2]{3,4,2,1,0:T(2,128)S(1)}, s32[1,1,1,16,2]{3,4,2,1,0:T(2,128)}, u32[]{:S(2)}) copy-start(s32[1,1,1,16,2]{3,4,2,1,0:T(2,128)} %param.14) | copy-start | bytes 388
  17.1 3.3 %copy-start.3 = (s32[1,1,16,2]{2,3,1,0:T(2,128)S(1)}, s32[1,1,16,2]{2,3,1,0:T(2,128)}, u32[]{:S(2)}) copy-start(s32[1,1,16,2]{2,3,1,0:T(2,128)} %param.19) | copy-start | bytes 388
  17.1 3.3 %copy-start.4 = (s32[1,1,1,48,2]{3,4,2,1,0:T(2,128)S(1)}, s32[1,1,1,48,2]{3,4,2,1,0:T(2,128)}, u32[]{:S(2)}) copy-start(s32[1,1,1,48,2]{3,4,2,1,0:T(2,128)} %param.17) | copy-start | bytes 1156
  21.5 2.7 %copy-start.1 = (bf16[1,1,1,16,2,128,128]{6,5,4,3,2,1,0:T(8,128)(2,1)S(1)}, bf16[1,1,1,16,2,128,128]{6,5,4,3,2,1,0:T(8,128)(2,1)}, u32[]{:S(2)}) copy-start(bf16[1,1,1,16,2,128,128]{6,5,4,3,2,1,0:T(8,128)(2,1)} %param.13) | copy-start | bytes 3145732
  28.5 7.2 %copy-start.5 = (s32[1,1,1,16]{3,2,1,0:T(1,128)S(1)}, s32[1,1,1,16]{3,2,1,0:T(1,128)}, u32[]{:S(2)}) copy-start(s32[1,1,1,16]{3,2,1,0:T(1,128)} %param.15) | copy-start | bytes 196
  46.5 33.0 %collective-permute-start = (s32[48,2]{1,0:T(8,128)S(1)}, s32[48,2]{1,0:T(8,128)S(1)}, u32[]{:S(2)}, u32[]{:S(2)}) collective-permute-start(s32[48,2]{1,0:T(8,128)S(1)} %copy.54), channel_id=1, source_target_pairs={{0,24},{8,0},{16,8},{24,16},{1,25},{9,1},{17,9},{25,17},{2,26},{10... | collective-permute-start | bytes 1160 | tf_op jit(solution)/shard_map/ppermute | solution.py:12
  90.7 7.4 %copy-start.6 = (f32[16,2,128,128,1]{3,1,4,2,0:T(2,128)S(1)}, f32[16,2,128,128,1]{3,1,4,2,0:T(2,128)}, u32[]{:S(2)}) copy-start(f32[16,2,128,128,1]{3,1,4,2,0:T(2,128)} %fusion.9) | copy-start | bytes 6291460
Sparse Core Ops, SparseCore 0:
  109.9 11.7 reduce-scatter.1
where the time goes:
time: 131 us
  waiting for transfers between devices  42.2 us (32%)
  local copies, waits for them, and re-layouts  31.9 us (24%)
  matrix products  29.6 us (23%)
  between operations  13.5 us (10%)
  starting transfers between devices  10.4 us (8%)
  other arithmetic  3.07 us (2%)
    ppermute x6, waiting for transfers between devices, passed_along(): return lax.ppermute(value, axis, pairs)  30.2 us
    dot_general x2, matrix products, panel_terms(): jnp.einsum('rtuv,rtuxz->rvxz', matches.astype(jnp.float32), products, pre...  20.7 us
    transpose x2, local copies, waits for them, and re-layouts, panel_terms(): jnp.einsum('rtxy,rtuyz->rtuxz', a_panel, chosen, preferred_element_type=j...  14.6 us
    reduce_scatter x1, waiting for transfers between devices, local(): lax.psum_scatter(partial_value, 'layer', scatter_dimension=0, tiled=True)  12 us
    gather x4, local copies, waits for them, and re-layouts, pick_rows(): jnp.take(panel, wanted, axis=0)  11.1 us
    ppermute x6, starting transfers between devices, passed_along(): return lax.ppermute(value, axis, pairs)  10.4 us
    dot_general x2, matrix products, panel_terms(): jnp.einsum('rtxy,rtuyz->rtuxz', a_panel, chosen, preferred_element_type=j...  8.96 us
  transfers between devices with their start and end apart: 7, of which 2 were waited for; matrix products, arithmetic and copies ran while one was open for 30% of the time, Pallas kernels for 0%

commit v1 on v0

--- a/solution.py
+++ b/solution.py
@@ -1,9 +1,17 @@
+import functools
+
 import jax
 import jax.numpy as jnp
 from jax import lax
+from jax.experimental import pallas as pl
+from jax.experimental.pallas import tpu as pltpu
 from jax.sharding import PartitionSpec as P
 
 STEPS = 2
+CAPACITY = 32
+CHUNKS = 4
+ABSENT = 1000
+LANES = 128
 
 
 def passed_along(value, axis, steps):
@@ -31,33 +39,313 @@
     )
 
 
-def local(a_blocks, a_cols, a_count, b_blocks, b_cols, b_count, c_cols):
-    a_panel = a_blocks[0, 0, 0]
-    a_index = a_cols[0, 0, 0]
-    a_live = a_count[0, 0, 0]
-    b_panel = b_blocks[0, 0, 0]
-    b_index = b_cols[0, 0, 0]
-    b_live = b_count[0, 0, 0]
-    out_cols = c_cols[0, 0]
+def general(a_panel, a_index, a_live, b_panel, b_index, b_live, out_cols):
     partial_value = jnp.zeros(
         (out_cols.shape[0], out_cols.shape[1], a_panel.shape[2], b_panel.shape[3]), jnp.float32
     )
     for cannon_step in range(STEPS):
         if cannon_step > 0:
             a_panel, a_index, a_live = passed_along((a_panel, a_index, a_live), "col", -1)
-        if cannon_step > 0:
             b_panel, b_index, b_live = passed_along((b_panel, b_index, b_live), "row", -1)
         chosen, chosen_cols, chosen_live = pick_rows(b_panel, b_index, b_live, a_index)
         partial_value = partial_value + panel_terms(
             a_panel, a_live, chosen, chosen_cols, chosen_live, out_cols
         )
     summed = lax.psum_scatter(partial_value, "layer", scatter_dimension=0, tiled=True)
-    return summed.astype(jnp.bfloat16)[None, None]
+    return summed.astype(jnp.bfloat16)
+
+
+def lists_of(a_cols, a_count, b_cols, b_count, c_cols):
+    rows, ka = a_cols.shape
+    kc = c_cols.shape[1]
+    panel, kb = b_cols.shape
+    stride = panel // rows
+    r = lax.broadcasted_iota(jnp.int32, (rows, ka), 0)
+    t = lax.broadcasted_iota(jnp.int32, (rows, ka), 1)
+    offset = (a_cols - stride * r + 1 + panel) % panel
+    offset = jnp.where(t < a_count[:, None], offset, ABSENT)
+    u = lax.broadcasted_iota(jnp.int32, (panel, kb), 1)
+    held = jnp.where(u < b_count[:, None], b_cols, -1)
+    near = jnp.roll(held, 1, axis=0).reshape(rows, stride * kb)
+    full = (rows, ka, kc)
+    parts = [jnp.broadcast_to(offset[:, :, None], full), jnp.broadcast_to(c_cols[:, None, :], full)]
+    parts += [jnp.broadcast_to(near[:, k, None, None], full) for k in range(stride * kb)]
+    tile = jnp.stack([part.reshape(-1) for part in parts])
+    return jnp.pad(tile, ((0, 0), (0, LANES - tile.shape[1])), constant_values=ABSENT)
+
+
+def matched(a_row, c_row, b_rows, rows, panel, kb):
+    shape = (8, LANES)
+    stride = panel // rows
+    lane = lax.broadcasted_iota(jnp.int32, shape, 1)
+    r = lane // 4
+    a_row = jnp.broadcast_to(a_row, shape)
+    c_row = jnp.broadcast_to(c_row, shape)
+    need = jnp.zeros(shape, jnp.int32)
+    place = jnp.full(shape, panel * kb, jnp.int32)
+    for d in range(stride):
+        m = r * stride + (d - 1)
+        m = jnp.where(m < 0, m + panel, m)
+        for u in range(kb):
+            k = d * kb + u
+            hit = (a_row == d) & (c_row == jnp.broadcast_to(b_rows[k : k + 1], shape))
+            hit = hit & (lane < rows * 4)
+            need = jnp.where(hit, 1, need)
+            place = jnp.where(hit, m * kb + u, place)
+    return need, place
+
+
+def earlier(need):
+    lane = lax.broadcasted_iota(jnp.int32, need.shape, 1)
+    total = need
+    step = 1
+    while step < LANES:
+        total = total + jnp.where(lane >= step, pltpu.roll(total, step, 1), 0)
+        step *= 2
+    return total - need
+
+
+def kernel(
+    n_row, n_col, panel, kb,
+    lists_ref, a_hbm, b_hbm,
+    out_ref, flag_ref,
+    av, bv, a_in, b_in, packed, part, layer_in, tiles, table_v, table_s, send_v, send_s,
+    flag_own, flag_layer, flag_row_src, flag_row, flag_col_src, flag_col,
+    local_sem, list_send, list_recv, a_send, a_recv, b_send, b_recv, l_send, l_recv,
+    f0_send, f0_recv, f1_send, f1_recv, f2_send, f2_recv,
+):
+    row = lax.axis_index("row")
+    col = lax.axis_index("col")
+    layer = lax.axis_index("layer")
+    rows = out_ref.shape[0] * 2
+    half = rows // 2
+
+    def at(d_row, d_col, d_layer=0):
+        return {
+            "row": lax.rem(row + d_row + n_row, n_row),
+            "col": lax.rem(col + d_col + n_col, n_col),
+            "layer": lax.rem(layer + d_layer, 2),
+        }
+
+    load_b = pltpu.make_async_copy(b_hbm, bv.at[pl.ds(0, panel * kb)], local_sem.at[0])
+    load_b.start()
+    load_a = pltpu.make_async_copy(a_hbm, av, local_sem.at[1])
+    load_a.start()
+
+    barrier = pltpu.get_barrier_semaphore()
+    partners = [at(o, 0) for o in range(1, n_row)] + [at(0, o) for o in range(1, n_col)]
+    partners += [at(0, 0, 1), at(1, -1), at(-1, 1)]
+    for partner in partners:
+        pl.semaphore_signal(barrier, inc=1, device_id=partner, device_id_type=pl.DeviceIdType.MESH)
+
+    zero = jnp.zeros(bv.shape[1:], bv.dtype)
+    bv[panel * kb] = zero
+    b_in[CAPACITY] = zero
+    own = lists_ref[...]
+    need, place = matched(own[0:1], own[1:2], own[2:], rows, panel, kb)
+    table_v[0] = place
+
+    pl.semaphore_wait(barrier, len(partners))
+
+    def remote(src, dst, send, recv, device):
+        copy = pltpu.make_async_remote_copy(
+            src_ref=src, dst_ref=dst, send_sem=send, recv_sem=recv,
+            device_id=device, device_id_type=pl.DeviceIdType.MESH,
+        )
+        copy.start()
+        return copy
+
+    sends = {}
+    for slot, device in ((2, at(1, 0)), (3, at(1, -1)), (1, at(-1, 0)), (0, at(0, -1))):
+        sends[slot] = remote(lists_ref, tiles.at[slot], list_send.at[slot], list_recv.at[slot], device)
+    a_copies = []
+    per = av.shape[0] // CHUNKS
+    for c in range(CHUNKS):
+        piece = pl.ds(c * per, per)
+        a_copies.append(
+            remote(a_hbm.at[piece], a_in.at[piece], a_send.at[c], a_recv.at[c], at(0, -1))
+        )
+
+    sends[2].wait_recv()
+    sends[3].wait_recv()
+    need, place = matched(tiles[3, 0:1], tiles[2, 1:2], own[2:], rows, panel, kb)
+    before = earlier(need)
+    wanted = lax.broadcasted_iota(jnp.int32, (CAPACITY, LANES), 0)
+    spread = (CAPACITY, LANES)
+    here = (jnp.broadcast_to(before[0:1], spread) == wanted) & (
+        jnp.broadcast_to(need[0:1], spread) > 0
+    )
+    chosen = jnp.sum(jnp.where(here, jnp.broadcast_to(place[0:1], spread), 0), axis=1, keepdims=True)
+    send_v[...] = jnp.broadcast_to(chosen, spread)
+    to_smem = pltpu.make_async_copy(send_v, send_s, local_sem.at[2])
+    to_smem.start()
+    lane = lax.broadcasted_iota(jnp.int32, (8, LANES), 1)
+    last = jnp.where(lane == LANES - 1, before + need, 0)
+    flag_own[...] = jnp.broadcast_to(jnp.max(last, axis=1, keepdims=True), (8, LANES))
+    load_b.wait()
+    to_smem.wait()
+    b_copies = []
+    per = CAPACITY // CHUNKS
+    for c in range(CHUNKS):
+        for k in range(c * per, (c + 1) * per):
+            packed[k] = bv[send_s[k, 0]]
+        piece = pl.ds(c * per, per)
+        b_copies.append(
+            remote(packed.at[piece], b_in.at[piece], b_send.at[c], b_recv.at[c], at(-1, 0))
+        )
+    f0 = remote(flag_own, flag_layer, f0_send.at[0], f0_recv.at[0], at(0, 0, 1))
+
+    sends[0].wait_recv()
+    sends[1].wait_recv()
+    need, place = matched(tiles[0, 0:1], own[1:2], tiles[1][2:], rows, panel, kb)
+    before = earlier(need)
+    table_v[1] = jnp.where((need > 0) & (before < CAPACITY), before, CAPACITY)
+    to_smem = pltpu.make_async_copy(table_v, table_s, local_sem.at[3])
+    to_smem.start()
+
+    f0.wait()
+    flag_row_src[...] = jnp.maximum(flag_own[...], flag_layer[...])
+    f1 = [
+        remote(flag_row_src, flag_row.at[o - 1], f1_send.at[o - 1], f1_recv.at[o - 1], at(o, 0))
+        for o in range(1, n_row)
+    ]
+    to_smem.wait()
+    load_a.wait()
+
+    def product(step, a, b, r):
+        block = [b[table_s[step, 0, 4 * r + k]] for k in range(4)]
+        left = jnp.concatenate([a[2 * r], a[2 * r + 1]], axis=1)
+        right = jnp.concatenate(
+            [jnp.concatenate(block[:2], axis=1), jnp.concatenate(block[2:], axis=1)], axis=0
+        )
+        return jnp.dot(left, right, preferred_element_type=jnp.float32)
+
+    @pl.loop(0, rows, unroll=4)
+    def _(r):
+        part[r] = product(0, av, bv, r)
+
+    worst = flag_row_src[...]
+    for o in range(1, n_row):
+        f1[o - 1].wait()
+        worst = jnp.maximum(worst, flag_row[o - 1])
+    flag_col_src[...] = worst
+    f2 = [
+        remote(flag_col_src, flag_col.at[o - 1], f2_send.at[o - 1], f2_recv.at[o - 1], at(0, o))
+        for o in range(1, n_col)
+    ]
+    for o in range(1, n_col):
+        f2[o - 1].wait()
+        worst = jnp.maximum(worst, flag_col[o - 1])
+    flag_ref[...] = worst
+
+    for copy in a_copies + b_copies:
+        copy.wait_recv()
+
+    theirs = (1 - layer) * half
+    mine = layer * half
+
+    l_copies = []
+    per = half // 2
+    for c in range(2):
+        @pl.loop(0, per, unroll=4)
+        def _(k):
+            r = theirs + c * per + k
+            part[r] += product(1, a_in, b_in, r)
+
+        l_copies.append(
+            remote(
+                part.at[pl.ds(theirs + c * per, per)], layer_in.at[pl.ds(c * per, per)],
+                l_send.at[c], l_recv.at[c], at(0, 0, 1),
+            )
+        )
+
+    @pl.loop(0, half, unroll=4)
+    def _(k):
+        r = mine + k
+        part[r] += product(1, a_in, b_in, r)
+
+    for c in range(2):
+        l_copies[c].wait_recv()
+
+        @pl.loop(0, per, unroll=2)
+        def _(k):
+            k = c * per + k
+            total = (part[mine + k] + layer_in[k]).astype(out_ref.dtype)
+            out_ref[k, 0] = total[:, : out_ref.shape[3]]
+            out_ref[k, 1] = total[:, out_ref.shape[3] :]
+
+    for copy in list(sends.values()) + a_copies + b_copies + l_copies:
+        copy.wait_send()
+
+
+def local(n_row, n_col, a_blocks, a_cols, a_count, b_blocks, b_cols, b_count, c_cols):
+    a_panel, a_index, a_live = a_blocks[0, 0, 0], a_cols[0, 0, 0], a_count[0, 0, 0]
+    b_panel, b_index, b_live = b_blocks[0, 0, 0], b_cols[0, 0, 0], b_count[0, 0, 0]
+    out_cols = c_cols[0, 0]
+    rows, ka, size, _ = a_panel.shape
+    panel, kb, _, width = b_panel.shape
+    kc = out_cols.shape[1]
+    half = rows // 2
+    lists = lists_of(a_index, a_live, b_index, b_live, out_cols)
+    vmem = pltpu.VMEM
+    dma = pltpu.SemaphoreType.DMA
+    tile = (8, LANES)
+    anywhere = pl.BlockSpec(memory_space=pl.ANY)
+    in_vmem = pl.BlockSpec(memory_space=vmem)
+    quick, worst = pl.pallas_call(
+        functools.partial(kernel, n_row, n_col, panel, kb),
+        out_shape=(
+            jax.ShapeDtypeStruct((half, kc, size, width), jnp.bfloat16),
+            jax.ShapeDtypeStruct(tile, jnp.int32),
+        ),
+        in_specs=[in_vmem, anywhere, anywhere],
+        out_specs=(in_vmem, in_vmem),
+        scratch_shapes=[
+            vmem((rows * ka, size, size), jnp.bfloat16),
+            vmem((panel * kb + 1, size, width), jnp.bfloat16),
+            vmem((rows * ka, size, size), jnp.bfloat16),
+            vmem((CAPACITY + 1, size, width), jnp.bfloat16),
+            vmem((CAPACITY, size, width), jnp.bfloat16),
+            vmem((rows, size, kc * width), jnp.float32),
+            vmem((half, size, kc * width), jnp.float32),
+            vmem((4,) + tile, jnp.int32),
+            vmem((2,) + tile, jnp.int32),
+            pltpu.SMEM((2,) + tile, jnp.int32),
+            vmem((CAPACITY, LANES), jnp.int32),
+            pltpu.SMEM((CAPACITY, LANES), jnp.int32),
+            vmem(tile, jnp.int32),
+            vmem(tile, jnp.int32),
+            vmem(tile, jnp.int32),
+            vmem((n_row - 1,) + tile, jnp.int32),
+            vmem(tile, jnp.int32),
+            vmem((n_col - 1,) + tile, jnp.int32),
+            dma((4,)),
+            dma((4,)), dma((4,)),
+            dma((CHUNKS,)), dma((CHUNKS,)),
+            dma((CHUNKS,)), dma((CHUNKS,)),
+            dma((2,)), dma((2,)),
+            dma((1,)), dma((1,)),
+            dma((n_row - 1,)), dma((n_row - 1,)),
+            dma((n_col - 1,)), dma((n_col - 1,)),
+        ],
+        compiler_params=pltpu.CompilerParams(
+            collective_id=0, has_side_effects=True, vmem_limit_bytes=40 * 1024 * 1024
+        ),
+        cost_estimate=pl.CostEstimate(
+            flops=4 * rows * size * ka * size * kc * width, bytes_accessed=6 << 20, transcendentals=0
+        ),
+    )(lists, a_panel.reshape(rows * ka, size, size), b_panel.reshape(panel * kb, size, width))
+    result = lax.cond(
+        worst[0, 0] > CAPACITY,
+        lambda: general(a_panel, a_index, a_live, b_panel, b_index, b_live, out_cols),
+        lambda: quick,
+    )
+    return result[None, None]
 
 
 def solution(mesh):
     return jax.shard_map(
-        local,
+        functools.partial(local, mesh.shape["row"], mesh.shape["col"]),
         mesh=mesh,
         in_specs=(
             P("row", "col", "layer", None, None, None, None),

time: 131 us -> 62.4 us (0.48)
  waiting for transfers between devices: 42.2 us -> 0 us
  Pallas kernels: 0 us -> 42 us
  matrix products: 29.6 us -> 0 us
  local copies, waits for them, and re-layouts: 31.9 us -> 4.24 us
  starting transfers between devices: 10.4 us -> 0 us
  other arithmetic: 3.07 us -> 1.48 us
    pallas_call x0 -> x1, Pallas kernels: none -> 42 us  [local(): pl.pallas_call(functools.partial(kernel, n_row, n_col, panel, kb), out_sh...]
    ppermute x6 -> x0, waiting for transfers between devices: 30.2 us -> none  [passed_along(): return lax.ppermute(value, axis, pairs)]
    dot_general x4 -> x0, matrix products: 29.6 us -> none  [the longest x2 20.7 us: panel_terms(): jnp.einsum('rtuv,rtuxz->rvxz', matches.astype(jnp.float32), products, pre...]
    transpose x2 -> x0, local copies, waits for them, and re-layouts: 14.6 us -> none  [panel_terms(): jnp.einsum('rtxy,rtuyz->rtuxz', a_panel, chosen, preferred_element_type=j...]
    gather x14 -> x0, local copies, waits for them, and re-layouts: 14.4 us -> none  [the longest x4 11.1 us: pick_rows(): jnp.take(panel, wanted, axis=0)]
    reduce_scatter x1 -> x0, waiting for transfers between devices: 12 us -> none  [local(): lax.psum_scatter(partial_value, 'layer', scatter_dimension=0, tiled=True)]
    ppermute x6 -> x0, starting transfers between devices: 10.4 us -> none  [passed_along(): return lax.ppermute(value, axis, pairs)]
    broadcast_in_dim x1 -> x0, other arithmetic: 2.11 us -> none  [local(): return summed.astype(jnp.bfloat16)[None, None]]
  transfers between devices with their start and end apart: 7 -> 0, of which waited for: 2 -> 0; matrix products, arithmetic and copies ran while one was open for 30% -> 0% of each run, Pallas kernels for 0% -> 0%
where the time goes in v1:
time: 62.4 us; the launch traced here: 62.2 us
  Pallas kernels  42 us (67%)
  between operations  14.2 us (23%)
  local copies, waits for them, and re-layouts  4.24 us (7%)
  other arithmetic  1.48 us (2%)
    pallas_call x1, Pallas kernels, local(): pl.pallas_call(functools.partial(kernel, n_row, n_col, panel, kb), out_sh...  42 us

profile of v1, /device:TPU:0, one launch (start us, length us, event | category | flops | bytes accessed | tf_op | source)
XLA Modules:
  0.0 62.2 jit_solution(16869013121955321697)
XLA Ops:
  6.5 0.7 %compare_select_fusion.3 = s32[16,2]{0,1:T(2,128)S(1)} fusion(s32[1,1,1,16,2]{3,4,2,1,0:T(2,128)} %param.16, s32[16]{0:T(128)S(1)} %iota_multiply_fusion, s32[16]{0:T(128)} %bitcast.83), kind=kLoop, calls=%fused_computation.53 | loop fusion | flops 320 | bytes 384 | tf_op jit(solution)/shard_map/jit(_where)/select_n | solution.py:66
  7.2 0.7 %compare_select_fusion.2 = s32[48,2]{0,1:T(2,128)S(1)} fusion(s32[48]{0:T(128)} %bitcast.66, s32[1,1,1,48,2]{3,4,2,1,0:T(2,128)} %param.19), kind=kLoop, calls=%fused_computation.51 | loop fusion | flops 192 | bytes 960 | tf_op jit(solution)/shard_map/jit(_where)/select_n | solution.py:68
  7.9 0.1 slice.29
  8.0 0.1 pad_add_fusion
  8.1 0.1 copy.84
  8.2 0.1 broadcast_in_dim.102
  8.2 0.1 stack_reshape.24
  8.4 0.8 %copy.85 = s32[16,2]{1,0:T(8,128)S(1)} copy(s32[16,2]{0,1:T(2,128)} %bitcast.80) | data formatting | bytes 256 | tf_op jit(solution)/shard_map/broadcast_in_dim | solution.py:71
  9.1 0.1 stack_reshape.25
  9.3 0.1 copy.86
  9.3 0.1 reshape.103
  9.4 0.3 slice_reduce_fusion
  9.7 0.1 broadcast_in_dim.117
  9.8 0.1 stack_reshape.31
  9.9 0.1 broadcast_in_dim.115
  10.0 0.1 stack_reshape.30
  10.1 0.1 broadcast_in_dim.113
  10.2 0.1 stack_reshape.29
  10.3 0.1 broadcast_in_dim.111
  10.4 0.1 stack_reshape.28
  10.5 0.1 broadcast_in_dim.109
  10.6 0.1 stack_reshape.27
  10.7 0.1 broadcast_in_dim.107
  10.8 0.1 stack_reshape.26
  10.9 0.0 copy-start
  11.0 0.0 copy-start.1
  11.0 0.0 copy-start.2
  11.0 0.0 copy-start.5
  11.0 42.0 %shard_map.75 = (bf16[8,2,128,128]{3,2,1,0:T(8,128)(2,1)S(1)}, s32[8,128]{1,0:T(8,128)S(1)}) custom-call(s32[8,128]{1,0:T(8,128)S(1)} %pad.4.lists_ref, bf16[32,128,128]{2,1,0:T(8,128)(2,1)} %bitcast.73, bf16[96,128,128]{2,1,0:T(8,128)(2,1)} %bitcast.68), custom_call_target="tpu_custom_call" | custom-call | flops 536870912 | bytes 6291456 | tf_op jit(solution)/shard_map/pallas_call | solution.py:295
  53.1 0.5 slice.37
  54.3 0.2 conditional.1
  54.5 0.8 %copy.99 = bf16[1,1,8,2,128,128]{5,4,3,2,1,0:T(8,128)(2,1)} copy(bf16[1,1,8,2,128,128]{5,4,3,2,1,0:T(8,128)(2,1)S(1)} %get-tuple-element.45) | data formatting | bytes 1048576
  (12 shorter events, 0.1 us)
Async XLA Ops:
  10.9 43.3 %copy-start = (s32[1,1,1,48]{3,2,1,0:T(1,128)S(1)}, s32[1,1,1,48]{3,2,1,0:T(1,128)}, u32[]{:S(2)}) copy-start(s32[1,1,1,48]{3,2,1,0:T(1,128)} %param.20) | copy-start | bytes 580
  11.0 43.3 %copy-start.1 = (bf16[1,1,1,48,2,128,128]{6,5,4,3,2,1,0:T(8,128)(2,1)S(1)}, bf16[1,1,1,48,2,128,128]{6,5,4,3,2,1,0:T(8,128)(2,1)}, u32[]{:S(2)}) copy-start(bf16[1,1,1,48,2,128,128]{6,5,4,3,2,1,0:T(8,128)(2,1)} %param.18) | copy-start | bytes 9437188
  11.0 43.3 %copy-start.2 = (s32[1,1,1,16,2]{3,4,2,1,0:T(2,128)S(1)}, s32[1,1,1,16,2]{3,4,2,1,0:T(2,128)}, u32[]{:S(2)}) copy-start(s32[1,1,1,16,2]{3,4,2,1,0:T(2,128)} %param.16) | copy-start | bytes 388
  11.0 43.3 %copy-start.3 = (s32[1,1,16,2]{2,3,1,0:T(2,128)S(1)}, s32[1,1,16,2]{2,3,1,0:T(2,128)}, u32[]{:S(2)}) copy-start(s32[1,1,16,2]{2,3,1,0:T(2,128)} %param.21) | copy-start | bytes 388
  11.0 43.3 %copy-start.4 = (s32[1,1,1,48,2]{3,4,2,1,0:T(2,128)S(1)}, s32[1,1,1,48,2]{3,4,2,1,0:T(2,128)}, u32[]{:S(2)}) copy-start(s32[1,1,1,48,2]{3,4,2,1,0:T(2,128)} %param.19) | copy-start | bytes 1156
  11.0 43.3 %copy-start.5 = (s32[1,1,1,16]{3,2,1,0:T(1,128)S(1)}, s32[1,1,1,16]{3,2,1,0:T(1,128)}, u32[]{:S(2)}) copy-start(s32[1,1,1,16]{3,2,1,0:T(1,128)} %param.17) | copy-start | bytes 196

commit v2 on v1

--- a/solution.py
+++ b/solution.py
@@ -7,71 +7,51 @@
 from jax.experimental.pallas import tpu as pltpu
 from jax.sharding import PartitionSpec as P
 
-STEPS = 2
 CAPACITY = 32
 CHUNKS = 4
 ABSENT = 1000
 LANES = 128
 
 
-def passed_along(value, axis, steps):
-    count = lax.axis_size(axis)
-    pairs = [(source, (source + steps) % count) for source in range(count)]
-    return lax.ppermute(value, axis, pairs)
-
-
-def pick_rows(panel, index, live, wanted):
-    return (
-        jnp.take(panel, wanted, axis=0),
-        jnp.take(index, wanted, axis=0),
-        jnp.take(live, wanted, axis=0),
-    )
-
-
-def panel_terms(a_panel, a_live, chosen, chosen_cols, chosen_live, out_cols):
-    slot_a = lax.broadcasted_iota(jnp.int32, chosen_cols.shape, 1)
-    slot_b = lax.broadcasted_iota(jnp.int32, chosen_cols.shape, 2)
-    usable = (slot_a < a_live[:, None, None]) & (slot_b < chosen_live[:, :, None])
-    matches = (chosen_cols[:, :, :, None] == out_cols[:, None, None, :]) & usable[:, :, :, None]
-    products = jnp.einsum("rtxy,rtuyz->rtuxz", a_panel, chosen, preferred_element_type=jnp.float32)
-    return jnp.einsum(
-        "rtuv,rtuxz->rvxz", matches.astype(jnp.float32), products, precision=lax.Precision.HIGHEST
-    )
-
-
-def general(a_panel, a_index, a_live, b_panel, b_index, b_live, out_cols):
-    partial_value = jnp.zeros(
-        (out_cols.shape[0], out_cols.shape[1], a_panel.shape[2], b_panel.shape[3]), jnp.float32
-    )
-    for cannon_step in range(STEPS):
-        if cannon_step > 0:
-            a_panel, a_index, a_live = passed_along((a_panel, a_index, a_live), "col", -1)
-            b_panel, b_index, b_live = passed_along((b_panel, b_index, b_live), "row", -1)
-        chosen, chosen_cols, chosen_live = pick_rows(b_panel, b_index, b_live, a_index)
-        partial_value = partial_value + panel_terms(
-            a_panel, a_live, chosen, chosen_cols, chosen_live, out_cols
-        )
-    summed = lax.psum_scatter(partial_value, "layer", scatter_dimension=0, tiled=True)
-    return summed.astype(jnp.bfloat16)
-
-
-def lists_of(a_cols, a_count, b_cols, b_count, c_cols):
-    rows, ka = a_cols.shape
-    kc = c_cols.shape[1]
-    panel, kb = b_cols.shape
+def fill_lists(tile_ref, rows_ref, a_cols, a_count, b_cols, b_count, c_cols):
+    ka, rows = a_cols.shape
+    kc = c_cols.shape[0]
+    kb, panel = b_cols.shape
     stride = panel // rows
-    r = lax.broadcasted_iota(jnp.int32, (rows, ka), 0)
-    t = lax.broadcasted_iota(jnp.int32, (rows, ka), 1)
-    offset = (a_cols - stride * r + 1 + panel) % panel
-    offset = jnp.where(t < a_count[:, None], offset, ABSENT)
-    u = lax.broadcasted_iota(jnp.int32, (panel, kb), 1)
-    held = jnp.where(u < b_count[:, None], b_cols, -1)
-    near = jnp.roll(held, 1, axis=0).reshape(rows, stride * kb)
-    full = (rows, ka, kc)
-    parts = [jnp.broadcast_to(offset[:, :, None], full), jnp.broadcast_to(c_cols[:, None, :], full)]
-    parts += [jnp.broadcast_to(near[:, k, None, None], full) for k in range(stride * kb)]
-    tile = jnp.stack([part.reshape(-1) for part in parts])
-    return jnp.pad(tile, ((0, 0), (0, LANES - tile.shape[1])), constant_values=ABSENT)
+    r = lax.broadcasted_iota(jnp.int32, (ka, rows), 1)
+    t = lax.broadcasted_iota(jnp.int32, (ka, rows), 0)
+    offset = a_cols[...] - stride * r + 1
+    offset = jnp.where(offset < 0, offset + panel, offset)
+    offset = jnp.where(offset >= panel, offset - panel, offset)
+    u = lax.broadcasted_iota(jnp.int32, (kb, panel), 0)
+    rows_ref[...] = jnp.full(rows_ref.shape, ABSENT, jnp.int32)
+    rows_ref[0:ka, 0:rows] = jnp.where(t < a_count[...], offset, ABSENT)
+    rows_ref[ka : ka + kc, 0:rows] = c_cols[...]
+    rows_ref[ka + kc : ka + kc + kb, 0:panel] = jnp.where(u < b_count[...], b_cols[...], -1)
+    columns = jnp.transpose(rows_ref[...])
+
+    def along(height, source, column):
+        place = lax.broadcasted_iota(jnp.int32, (height, LANES), 0)
+        entries = jnp.broadcast_to(columns[:height, column : column + 1], (height, LANES))
+        return jnp.sum(jnp.where(place == source(height), entries, 0), axis=0, keepdims=True)
+
+    def own_row(height):
+        return lax.broadcasted_iota(jnp.int32, (height, LANES), 1) // 4
+
+    lane = lax.broadcasted_iota(jnp.int32, (1, LANES), 1)
+    a_slots = [along(rows, own_row, k) for k in range(ka)]
+    c_slots = [along(rows, own_row, ka + k) for k in range(kc)]
+    tile_ref[0:1] = jnp.where(lane % 4 < 2, a_slots[0], a_slots[1])
+    tile_ref[1:2] = jnp.where(lane % 2 == 0, c_slots[0], c_slots[1])
+    for d in range(stride):
+
+        def near(height):
+            m = own_row(height) * stride + (d - 1)
+            return jnp.where(m < 0, m + panel, m)
+
+        for k in range(kb):
+            row = 2 + d * kb + k
+            tile_ref[row : row + 1] = along(panel, near, ka + kc + k)
 
 
 def matched(a_row, c_row, b_rows, rows, panel, kb):
@@ -106,9 +86,10 @@
 
 
 def kernel(
-    n_row, n_col, panel, kb,
-    lists_ref, a_hbm, b_hbm,
+    n_row, n_col, capacity,
+    a_cols, a_count, b_cols, b_count, c_cols, a_hbm, b_hbm,
     out_ref, flag_ref,
+    lists_ref, rows_ref,
     av, bv, a_in, b_in, packed, part, layer_in, tiles, table_v, table_s, send_v, send_s,
     flag_own, flag_layer, flag_row_src, flag_row, flag_col_src, flag_col,
     local_sem, list_send, list_recv, a_send, a_recv, b_send, b_recv, l_send, l_recv,
@@ -119,6 +100,7 @@
     layer = lax.axis_index("layer")
     rows = out_ref.shape[0] * 2
     half = rows // 2
+    kb, panel = b_cols.shape
 
     def at(d_row, d_col, d_layer=0):
         return {
@@ -140,7 +122,8 @@
 
     zero = jnp.zeros(bv.shape[1:], bv.dtype)
     bv[panel * kb] = zero
-    b_in[CAPACITY] = zero
+    b_in[capacity] = zero
+    fill_lists(lists_ref, rows_ref, a_cols, a_count, b_cols, b_count, c_cols)
     own = lists_ref[...]
     need, place = matched(own[0:1], own[1:2], own[2:], rows, panel, kb)
     table_v[0] = place
@@ -170,8 +153,8 @@
     sends[3].wait_recv()
     need, place = matched(tiles[3, 0:1], tiles[2, 1:2], own[2:], rows, panel, kb)
     before = earlier(need)
-    wanted = lax.broadcasted_iota(jnp.int32, (CAPACITY, LANES), 0)
-    spread = (CAPACITY, LANES)
+    wanted = lax.broadcasted_iota(jnp.int32, (capacity, LANES), 0)
+    spread = (capacity, LANES)
     here = (jnp.broadcast_to(before[0:1], spread) == wanted) & (
         jnp.broadcast_to(need[0:1], spread) > 0
     )
@@ -185,7 +168,7 @@
     load_b.wait()
     to_smem.wait()
     b_copies = []
-    per = CAPACITY // CHUNKS
+    per = capacity // CHUNKS
     for c in range(CHUNKS):
         for k in range(c * per, (c + 1) * per):
             packed[k] = bv[send_s[k, 0]]
@@ -199,7 +182,7 @@
     sends[1].wait_recv()
     need, place = matched(tiles[0, 0:1], own[1:2], tiles[1][2:], rows, panel, kb)
     before = earlier(need)
-    table_v[1] = jnp.where((need > 0) & (before < CAPACITY), before, CAPACITY)
+    table_v[1] = jnp.where((need > 0) & (before < capacity), before, capacity)
     to_smem = pltpu.make_async_copy(table_v, table_s, local_sem.at[3])
     to_smem.start()
 
@@ -236,7 +219,7 @@
     for o in range(1, n_col):
         f2[o - 1].wait()
         worst = jnp.maximum(worst, flag_col[o - 1])
-    flag_ref[...] = worst
+    flag_ref[...] = jnp.where(worst[0:1, 0:1] > capacity, 1, 0)
 
     for copy in a_copies + b_copies:
         copy.wait_recv()
@@ -278,41 +261,40 @@
         copy.wait_send()
 
 
-def local(n_row, n_col, a_blocks, a_cols, a_count, b_blocks, b_cols, b_count, c_cols):
-    a_panel, a_index, a_live = a_blocks[0, 0, 0], a_cols[0, 0, 0], a_count[0, 0, 0]
-    b_panel, b_index, b_live = b_blocks[0, 0, 0], b_cols[0, 0, 0], b_count[0, 0, 0]
-    out_cols = c_cols[0, 0]
-    rows, ka, size, _ = a_panel.shape
-    panel, kb, _, width = b_panel.shape
-    kc = out_cols.shape[1]
+def call(n_row, n_col, capacity, collective_id, a_cols, a_count, b_cols, b_count, c_cols, a, b):
+    ka, rows = a_cols.shape
+    kb, panel = b_cols.shape
+    kc = c_cols.shape[0]
+    size, width = a.shape[1], b.shape[2]
     half = rows // 2
-    lists = lists_of(a_index, a_live, b_index, b_live, out_cols)
     vmem = pltpu.VMEM
     dma = pltpu.SemaphoreType.DMA
     tile = (8, LANES)
     anywhere = pl.BlockSpec(memory_space=pl.ANY)
     in_vmem = pl.BlockSpec(memory_space=vmem)
-    quick, worst = pl.pallas_call(
-        functools.partial(kernel, n_row, n_col, panel, kb),
+    return pl.pallas_call(
+        functools.partial(kernel, n_row, n_col, capacity),
         out_shape=(
             jax.ShapeDtypeStruct((half, kc, size, width), jnp.bfloat16),
-            jax.ShapeDtypeStruct(tile, jnp.int32),
+            jax.ShapeDtypeStruct((1, 1), jnp.int32),
         ),
-        in_specs=[in_vmem, anywhere, anywhere],
+        in_specs=[in_vmem] * 5 + [anywhere] * 2,
         out_specs=(in_vmem, in_vmem),
         scratch_shapes=[
+            vmem(tile, jnp.int32),
+            vmem(tile, jnp.int32),
             vmem((rows * ka, size, size), jnp.bfloat16),
             vmem((panel * kb + 1, size, width), jnp.bfloat16),
             vmem((rows * ka, size, size), jnp.bfloat16),
-            vmem((CAPACITY + 1, size, width), jnp.bfloat16),
-            vmem((CAPACITY, size, width), jnp.bfloat16),
+            vmem((capacity + 1, size, width), jnp.bfloat16),
+            vmem((capacity, size, width), jnp.bfloat16),
             vmem((rows, size, kc * width), jnp.float32),
             vmem((half, size, kc * width), jnp.float32),
             vmem((4,) + tile, jnp.int32),
             vmem((2,) + tile, jnp.int32),
             pltpu.SMEM((2,) + tile, jnp.int32),
-            vmem((CAPACITY, LANES), jnp.int32),
-            pltpu.SMEM((CAPACITY, LANES), jnp.int32),
+            vmem((capacity, LANES), jnp.int32),
+            pltpu.SMEM((capacity, LANES), jnp.int32),
             vmem(tile, jnp.int32),
             vmem(tile, jnp.int32),
             vmem(tile, jnp.int32),
@@ -329,16 +311,27 @@
             dma((n_col - 1,)), dma((n_col - 1,)),
         ],
         compiler_params=pltpu.CompilerParams(
-            collective_id=0, has_side_effects=True, vmem_limit_bytes=40 * 1024 * 1024
+            collective_id=collective_id, has_side_effects=True, vmem_limit_bytes=40 * 1024 * 1024
         ),
         cost_estimate=pl.CostEstimate(
             flops=4 * rows * size * ka * size * kc * width, bytes_accessed=6 << 20, transcendentals=0
         ),
-    )(lists, a_panel.reshape(rows * ka, size, size), b_panel.reshape(panel * kb, size, width))
+    )(a_cols, a_count, b_cols, b_count, c_cols, a, b)
+
+
+def local(n_row, n_col, a_blocks, a_cols, a_count, b_blocks, b_cols, b_count, c_cols):
+    a_panel, b_panel = a_blocks[0, 0, 0], b_blocks[0, 0, 0]
+    args = (
+        a_cols[0, 0, 0].T, a_count[0, 0], b_cols[0, 0, 0].T, b_count[0, 0], c_cols[0, 0].T,
+        a_panel.reshape((-1,) + a_panel.shape[2:]), b_panel.reshape((-1,) + b_panel.shape[2:]),
+    )
+    every = a_panel.shape[0] * a_panel.shape[1] * c_cols.shape[3]
+    quick, over = call(n_row, n_col, CAPACITY, 0, *args)
     result = lax.cond(
-        worst[0, 0] > CAPACITY,
-        lambda: general(a_panel, a_index, a_live, b_panel, b_index, b_live, out_cols),
-        lambda: quick,
+        over[0, 0] > 0,
+        lambda args, quick: call(n_row, n_col, every, 1, *args)[0],
+        lambda args, quick: quick,
+        args, quick,
     )
     return result[None, None]
 

time: 62.4 us -> 45.1 us (0.72)
  between operations: 14.2 us -> 0.73 us
  local copies, waits for them, and re-layouts: 4.24 us -> 0.82 us
  other arithmetic: 1.48 us -> 0 us
  Pallas kernels: 42 us -> 43.4 us
    select_n x2 -> x0, other arithmetic: 1.39 us -> none  [the longest x1 0.7 us: lists_of(): held = jnp.where(u < b_count[:, None], b_cols, -1)]
    pallas_call x1, Pallas kernels: 42 us -> 43.4 us  [call(): pl.pallas_call(functools.partial(kernel, n_row, n_col, capacity), out_sha...]
    broadcast_in_dim x9 -> x0, local copies, waits for them, and re-layouts: 1.28 us -> none  [the longest x2 0.77 us: lists_of(): jnp.broadcast_to(c_cols[:, None, :], full)]
    another operation x9 -> x0, local copies, waits for them, and re-layouts: 1.02 us -> none  [lists_of(): tile = jnp.stack([part.reshape(-1) for part in parts])]
    slice x3 -> x0, local copies, waits for them, and re-layouts: 0.85 us -> none  [the longest x1 0.51 us: local(): worst[0, 0] > CAPACITY]
where the time goes in v2:
time: 45.1 us; the launch traced here: 44.9 us
  Pallas kernels  43.4 us (96%)
  local copies, waits for them, and re-layouts  0.82 us (2%)
  between operations  0.73 us (2%)
    pallas_call x1, Pallas kernels, call(): pl.pallas_call(functools.partial(kernel, n_row, n_col, capacity), out_sha...  43.4 us

profile of v2, /device:TPU:0, one launch (start us, length us, event | category | flops | bytes accessed | tf_op | source)
XLA Modules:
  0.0 44.9 jit_solution(4739457058796533026)
XLA Ops:
  0.0 0.0 copy-start.4
  0.0 0.0 copy-start.6
  0.0 0.0 copy-start.3
  0.0 0.0 copy-start
  0.0 0.0 copy-start.5
  0.0 0.0 copy-start.2
  0.0 0.0 copy-start.1
  0.0 43.4 %shard_map.75 = (bf16[8,2,128,128]{3,2,1,0:T(8,128)(2,1)S(1)}, s32[1,1]{1,0:T(1,128)}) custom-call(s32[2,16]{1,0:T(2,128)} %bitcast.22, s32[1,16]{1,0:T(1,128)} %bitcast.28, s32[2,48]{1,0:T(2,128)} %bitcast.24, s32[1,48]{1,0:T(1,128)} %bitcast.30, s32[2,16]{1,0:T(2,128)} %bitcast.26, bf16[32,128,128]{2,1,0:T(8,128)(2,1)} %bitcast.18, ...), custom_call_target="tpu_custom_call" | custom-call | flops 536870912 | bytes 6291456 | tf_op jit(solution)/shard_map/pallas_call | solution.py:275
  44.1 0.0 copy-done.4
  44.1 0.0 copy-done.6
  44.1 0.0 copy-done.3
  44.1 0.0 copy-done
  44.1 0.0 copy-done.5
  44.1 0.0 copy-done.2
  44.1 0.0 copy-done.1
  44.2 0.8 %copy.14 = bf16[1,1,8,2,128,128]{5,4,3,2,1,0:T(8,128)(2,1)} copy(bf16[1,1,8,2,128,128]{5,4,3,2,1,0:T(8,128)(2,1)S(1)} %get-tuple-element.37) | data formatting | bytes 1048576
  (1 shorter events, 0.0 us)
Async XLA Ops:
  0.0 44.1 %copy-start.4 = (s32[1,1,16,2]{2,3,1,0:T(2,128)S(1)}, s32[1,1,16,2]{2,3,1,0:T(2,128)}, u32[]{:S(2)}) copy-start(s32[1,1,16,2]{2,3,1,0:T(2,128)} %param.15) | copy-start | bytes 388
  0.0 44.1 %copy-start.6 = (s32[1,1,1,48]{3,2,1,0:T(1,128)S(1)}, s32[1,1,1,48]{3,2,1,0:T(1,128)}, u32[]{:S(2)}) copy-start(s32[1,1,1,48]{3,2,1,0:T(1,128)} %param.14) | copy-start | bytes 580
  0.0 44.1 %copy-start.3 = (s32[1,1,1,48,2]{3,4,2,1,0:T(2,128)S(1)}, s32[1,1,1,48,2]{3,4,2,1,0:T(2,128)}, u32[]{:S(2)}) copy-start(s32[1,1,1,48,2]{3,4,2,1,0:T(2,128)} %param.13) | copy-start | bytes 1156
  0.0 44.1 %copy-start = (bf16[1,1,1,48,2,128,128]{6,5,4,3,2,1,0:T(8,128)(2,1)S(1)}, bf16[1,1,1,48,2,128,128]{6,5,4,3,2,1,0:T(8,128)(2,1)}, u32[]{:S(2)}) copy-start(bf16[1,1,1,48,2,128,128]{6,5,4,3,2,1,0:T(8,128)(2,1)} %param.12) | copy-start | bytes 9437188
  0.0 44.1 %copy-start.5 = (s32[1,1,1,16]{3,2,1,0:T(1,128)S(1)}, s32[1,1,1,16]{3,2,1,0:T(1,128)}, u32[]{:S(2)}) copy-start(s32[1,1,1,16]{3,2,1,0:T(1,128)} %param.11) | copy-start | bytes 196
  0.0 44.1 %copy-start.2 = (s32[1,1,1,16,2]{3,4,2,1,0:T(2,128)S(1)}, s32[1,1,1,16,2]{3,4,2,1,0:T(2,128)}, u32[]{:S(2)}) copy-start(s32[1,1,1,16,2]{3,4,2,1,0:T(2,128)} %param.10) | copy-start | bytes 388
  0.0 44.1 %copy-start.1 = (bf16[1,1,1,16,2,128,128]{6,5,4,3,2,1,0:T(8,128)(2,1)S(1)}, bf16[1,1,1,16,2,128,128]{6,5,4,3,2,1,0:T(8,128)(2,1)}, u32[]{:S(2)}) copy-start(bf16[1,1,1,16,2,128,128]{6,5,4,3,2,1,0:T(8,128)(2,1)} %param.9) | copy-start | bytes 3145732

commit v3 on v2

--- a/solution.py
+++ b/solution.py
@@ -11,6 +11,11 @@
 CHUNKS = 4
 ABSENT = 1000
 LANES = 128
+
+
+def block_row(lane, rows):
+    q = lane // 4
+    return (q % 2) * (rows // 2) + q // 2
 
 
 def fill_lists(tile_ref, rows_ref, a_cols, a_count, b_cols, b_count, c_cols):
@@ -36,7 +41,7 @@
         return jnp.sum(jnp.where(place == source(height), entries, 0), axis=0, keepdims=True)
 
     def own_row(height):
-        return lax.broadcasted_iota(jnp.int32, (height, LANES), 1) // 4
+        return block_row(lax.broadcasted_iota(jnp.int32, (height, LANES), 1), rows)
 
     lane = lax.broadcasted_iota(jnp.int32, (1, LANES), 1)
     a_slots = [along(rows, own_row, k) for k in range(ka)]
@@ -58,7 +63,7 @@
     shape = (8, LANES)
     stride = panel // rows
     lane = lax.broadcasted_iota(jnp.int32, shape, 1)
-    r = lane // 4
+    r = block_row(lane, rows)
     a_row = jnp.broadcast_to(a_row, shape)
     c_row = jnp.broadcast_to(c_row, shape)
     need = jnp.zeros(shape, jnp.int32)
@@ -87,10 +92,11 @@
 
 def kernel(
     n_row, n_col, capacity,
-    a_cols, a_count, b_cols, b_count, c_cols, a_hbm, b_hbm,
+    a_cols_hbm, a_count_hbm, b_cols_hbm, b_count_hbm, c_cols_hbm, a_hbm, b_hbm,
     out_ref, flag_ref,
+    a_cols, a_count, b_cols, b_count, c_cols,
     lists_ref, rows_ref,
-    av, bv, a_in, b_in, packed, part, layer_in, tiles, table_v, table_s, send_v, send_s,
+    av, bv, a_in, b_first, b_last, packed, part, layer_in, tiles, table_v, table_s, send_v, send_s,
     flag_own, flag_layer, flag_row_src, flag_row, flag_col_src, flag_col,
     local_sem, list_send, list_recv, a_send, a_recv, b_send, b_recv, l_send, l_recv,
     f0_send, f0_recv, f1_send, f1_recv, f2_send, f2_recv,
@@ -109,24 +115,37 @@
             "layer": lax.rem(layer + d_layer, 2),
         }
 
-    load_b = pltpu.make_async_copy(b_hbm, bv.at[pl.ds(0, panel * kb)], local_sem.at[0])
-    load_b.start()
-    load_a = pltpu.make_async_copy(a_hbm, av, local_sem.at[1])
-    load_a.start()
-
     barrier = pltpu.get_barrier_semaphore()
     partners = [at(o, 0) for o in range(1, n_row)] + [at(0, o) for o in range(1, n_col)]
     partners += [at(0, 0, 1), at(1, -1), at(-1, 1)]
     for partner in partners:
         pl.semaphore_signal(barrier, inc=1, device_id=partner, device_id_type=pl.DeviceIdType.MESH)
 
+    loads = [
+        pltpu.make_async_copy(src, dst, local_sem.at[4 + k])
+        for k, (src, dst) in enumerate((
+            (a_cols_hbm, a_cols), (a_count_hbm, a_count), (b_cols_hbm, b_cols),
+            (b_count_hbm, b_count), (c_cols_hbm, c_cols),
+        ))
+    ]
+    for load in loads:
+        load.start()
+    load_b = pltpu.make_async_copy(b_hbm, bv.at[pl.ds(0, panel * kb)], local_sem.at[0])
+    load_b.start()
+    load_a = pltpu.make_async_copy(a_hbm, av, local_sem.at[1])
+    load_a.start()
+    per = capacity // CHUNKS
+    first = capacity - per
     zero = jnp.zeros(bv.shape[1:], bv.dtype)
     bv[panel * kb] = zero
-    b_in[capacity] = zero
+    b_first[first] = zero
+    b_last[per] = zero
+    for load in loads:
+        load.wait()
     fill_lists(lists_ref, rows_ref, a_cols, a_count, b_cols, b_count, c_cols)
     own = lists_ref[...]
     need, place = matched(own[0:1], own[1:2], own[2:], rows, panel, kb)
-    table_v[0] = place
+    table_v[0:1] = place[0:1]
 
     pl.semaphore_wait(barrier, len(partners))
 
@@ -142,9 +161,9 @@
     for slot, device in ((2, at(1, 0)), (3, at(1, -1)), (1, at(-1, 0)), (0, at(0, -1))):
         sends[slot] = remote(lists_ref, tiles.at[slot], list_send.at[slot], list_recv.at[slot], device)
     a_copies = []
-    per = av.shape[0] // CHUNKS
+    a_per = av.shape[0] // CHUNKS
     for c in range(CHUNKS):
-        piece = pl.ds(c * per, per)
+        piece = pl.ds(c * a_per, a_per)
         a_copies.append(
             remote(a_hbm.at[piece], a_in.at[piece], a_send.at[c], a_recv.at[c], at(0, -1))
         )
@@ -152,29 +171,28 @@
     sends[2].wait_recv()
     sends[3].wait_recv()
     need, place = matched(tiles[3, 0:1], tiles[2, 1:2], own[2:], rows, panel, kb)
-    before = earlier(need)
-    wanted = lax.broadcasted_iota(jnp.int32, (capacity, LANES), 0)
-    spread = (capacity, LANES)
-    here = (jnp.broadcast_to(before[0:1], spread) == wanted) & (
-        jnp.broadcast_to(need[0:1], spread) > 0
-    )
-    chosen = jnp.sum(jnp.where(here, jnp.broadcast_to(place[0:1], spread), 0), axis=1, keepdims=True)
-    send_v[...] = jnp.broadcast_to(chosen, spread)
+    spread = (rows * 4, LANES)
+    lane = lax.broadcasted_iota(jnp.int32, spread, 1)
+    entry = lax.broadcasted_iota(jnp.int32, spread, 0)
+    needed = jnp.broadcast_to(need[0:1], spread)
+    before = jnp.sum(jnp.where(lane < entry, needed, 0), axis=1, keepdims=True)
+    taken = jnp.where(lane == entry, needed * (1 + jnp.broadcast_to(place[0:1], spread)), 0)
+    taken = jnp.broadcast_to(jnp.sum(taken, axis=1, keepdims=True), spread)
+    here = (jnp.broadcast_to(before, spread) == lane) & (taken > 0)
+    send_v[...] = jnp.sum(jnp.where(here, taken - 1, 0), axis=0, keepdims=True)
     to_smem = pltpu.make_async_copy(send_v, send_s, local_sem.at[2])
     to_smem.start()
-    lane = lax.broadcasted_iota(jnp.int32, (8, LANES), 1)
-    last = jnp.where(lane == LANES - 1, before + need, 0)
-    flag_own[...] = jnp.broadcast_to(jnp.max(last, axis=1, keepdims=True), (8, LANES))
+    flag_own[...] = jnp.broadcast_to(jnp.sum(need, axis=1, keepdims=True), flag_own.shape)
     load_b.wait()
     to_smem.wait()
     b_copies = []
-    per = capacity // CHUNKS
     for c in range(CHUNKS):
         for k in range(c * per, (c + 1) * per):
-            packed[k] = bv[send_s[k, 0]]
+            packed[k] = bv[send_s[0, k]]
         piece = pl.ds(c * per, per)
+        landing = b_first.at[piece] if c < CHUNKS - 1 else b_last.at[pl.ds(0, per)]
         b_copies.append(
-            remote(packed.at[piece], b_in.at[piece], b_send.at[c], b_recv.at[c], at(-1, 0))
+            remote(packed.at[piece], landing, b_send.at[c], b_recv.at[c], at(-1, 0))
         )
     f0 = remote(flag_own, flag_layer, f0_send.at[0], f0_recv.at[0], at(0, 0, 1))
 
@@ -182,7 +200,7 @@
     sends[1].wait_recv()
     need, place = matched(tiles[0, 0:1], own[1:2], tiles[1][2:], rows, panel, kb)
     before = earlier(need)
-    table_v[1] = jnp.where((need > 0) & (before < capacity), before, capacity)
+    table_v[1:2] = jnp.where((need > 0) & (before < capacity), before, capacity)[0:1]
     to_smem = pltpu.make_async_copy(table_v, table_s, local_sem.at[3])
     to_smem.start()
 
@@ -195,8 +213,18 @@
     to_smem.wait()
     load_a.wait()
 
-    def product(step, a, b, r):
-        block = [b[table_s[step, 0, 4 * r + k]] for k in range(4)]
+    def blocks_of(step, r):
+        q = 2 * lax.rem(r, half) + r // half
+        return [table_s[step, 4 * q + k] for k in range(4)]
+
+    def from_first(place):
+        return b_first[jnp.where(place < first, place, first)]
+
+    def from_all(place):
+        last = jnp.where(place < first, per, place - first)
+        return jnp.where(place < first, from_first(place), b_last[last])
+
+    def product(a, block, r):
         left = jnp.concatenate([a[2 * r], a[2 * r + 1]], axis=1)
         right = jnp.concatenate(
             [jnp.concatenate(block[:2], axis=1), jnp.concatenate(block[2:], axis=1)], axis=0
@@ -205,7 +233,7 @@
 
     @pl.loop(0, rows, unroll=4)
     def _(r):
-        part[r] = product(0, av, bv, r)
+        part[r] = product(av, [bv[place] for place in blocks_of(0, r)], r)
 
     worst = flag_row_src[...]
     for o in range(1, n_row):
@@ -221,38 +249,45 @@
         worst = jnp.maximum(worst, flag_col[o - 1])
     flag_ref[...] = jnp.where(worst[0:1, 0:1] > capacity, 1, 0)
 
-    for copy in a_copies + b_copies:
-        copy.wait_recv()
-
     theirs = (1 - layer) * half
     mine = layer * half
-
+    early = first // 8
+    middle = (early + half + 1) // 2
     l_copies = []
-    per = half // 2
-    for c in range(2):
-        @pl.loop(0, per, unroll=4)
+
+    def add_step(base, low, high, read):
+        @pl.loop(low, high, unroll=high - low)
         def _(k):
-            r = theirs + c * per + k
-            part[r] += product(1, a_in, b_in, r)
-
+            r = base + k
+            part[r] += product(a_in, [read(place) for place in blocks_of(1, r)], r)
+
+    def hand_over(low, high):
+        c = len(l_copies)
         l_copies.append(
             remote(
-                part.at[pl.ds(theirs + c * per, per)], layer_in.at[pl.ds(c * per, per)],
+                part.at[pl.ds(theirs + low, high - low)], layer_in.at[pl.ds(low, high - low)],
                 l_send.at[c], l_recv.at[c], at(0, 0, 1),
             )
         )
 
-    @pl.loop(0, half, unroll=4)
-    def _(k):
-        r = mine + k
-        part[r] += product(1, a_in, b_in, r)
-
-    for c in range(2):
-        l_copies[c].wait_recv()
-
-        @pl.loop(0, per, unroll=2)
+    for copy in a_copies + b_copies[:-1]:
+        copy.wait_recv()
+    add_step(theirs, 0, early, from_first)
+    hand_over(0, early)
+    add_step(mine, 0, early, from_first)
+
+    b_copies[-1].wait_recv()
+    add_step(theirs, early, middle, from_all)
+    hand_over(early, middle)
+    add_step(theirs, middle, half, from_all)
+    hand_over(middle, half)
+    add_step(mine, early, half, from_all)
+
+    for copy, (low, high) in zip(l_copies, ((0, early), (early, middle), (middle, half))):
+        copy.wait_recv()
+
+        @pl.loop(low, high, unroll=high - low)
         def _(k):
-            k = c * per + k
             total = (part[mine + k] + layer_in[k]).astype(out_ref.dtype)
             out_ref[k, 0] = total[:, : out_ref.shape[3]]
             out_ref[k, 1] = total[:, out_ref.shape[3] :]
@@ -267,6 +302,7 @@
     kc = c_cols.shape[0]
     size, width = a.shape[1], b.shape[2]
     half = rows // 2
+    per = capacity // CHUNKS
     vmem = pltpu.VMEM
     dma = pltpu.SemaphoreType.DMA
     tile = (8, LANES)
@@ -278,34 +314,40 @@
             jax.ShapeDtypeStruct((half, kc, size, width), jnp.bfloat16),
             jax.ShapeDtypeStruct((1, 1), jnp.int32),
         ),
-        in_specs=[in_vmem] * 5 + [anywhere] * 2,
+        in_specs=[anywhere] * 7,
         out_specs=(in_vmem, in_vmem),
         scratch_shapes=[
+            vmem(a_cols.shape, jnp.int32),
+            vmem(a_count.shape, jnp.int32),
+            vmem(b_cols.shape, jnp.int32),
+            vmem(b_count.shape, jnp.int32),
+            vmem(c_cols.shape, jnp.int32),
             vmem(tile, jnp.int32),
             vmem(tile, jnp.int32),
             vmem((rows * ka, size, size), jnp.bfloat16),
             vmem((panel * kb + 1, size, width), jnp.bfloat16),
             vmem((rows * ka, size, size), jnp.bfloat16),
-            vmem((capacity + 1, size, width), jnp.bfloat16),
+            vmem((capacity - per + 1, size, width), jnp.bfloat16),
+            vmem((per + 1, size, width), jnp.bfloat16),
             vmem((capacity, size, width), jnp.bfloat16),
             vmem((rows, size, kc * width), jnp.float32),
             vmem((half, size, kc * width), jnp.float32),
             vmem((4,) + tile, jnp.int32),
-            vmem((2,) + tile, jnp.int32),
-            pltpu.SMEM((2,) + tile, jnp.int32),
-            vmem((capacity, LANES), jnp.int32),
-            pltpu.SMEM((capacity, LANES), jnp.int32),
+            vmem((2, LANES), jnp.int32),
+            pltpu.SMEM((2, LANES), jnp.int32),
+            vmem((1, LANES), jnp.int32),
+            pltpu.SMEM((1, LANES), jnp.int32),
             vmem(tile, jnp.int32),
             vmem(tile, jnp.int32),
             vmem(tile, jnp.int32),
             vmem((n_row - 1,) + tile, jnp.int32),
             vmem(tile, jnp.int32),
             vmem((n_col - 1,) + tile, jnp.int32),
-            dma((4,)),
+            dma((9,)),
             dma((4,)), dma((4,)),
             dma((CHUNKS,)), dma((CHUNKS,)),
             dma((CHUNKS,)), dma((CHUNKS,)),
-            dma((2,)), dma((2,)),
+            dma((3,)), dma((3,)),
             dma((1,)), dma((1,)),
             dma((n_row - 1,)), dma((n_row - 1,)),
             dma((n_col - 1,)), dma((n_col - 1,)),

time: 45.1 us -> 43.6 us (0.967)
  Pallas kernels: 43.4 us -> 41.9 us
    pallas_call x1, Pallas kernels: 43.4 us -> 41.9 us  [call(): pl.pallas_call(functools.partial(kernel, n_row, n_col, capacity), out_sha...]
where the time goes in v3:
time: 43.6 us; the launch traced here: 43.5 us
  Pallas kernels  41.9 us (96%)
  local copies, waits for them, and re-layouts  0.82 us (2%)
  between operations  0.73 us (2%)
    pallas_call x1, Pallas kernels, call(): pl.pallas_call(functools.partial(kernel, n_row, n_col, capacity), out_sha...  41.9 us

profile of v3, /device:TPU:0, one launch (start us, length us, event | category | flops | bytes accessed | tf_op | source)
XLA Modules:
  0.0 43.5 jit_solution(1752026821765595088)
XLA Ops:
  0.0 0.0 copy-start.4
  0.0 0.0 copy-start.6
  0.0 0.0 copy-start.3
  0.0 0.0 copy-start
  0.0 0.0 copy-start.5
  0.0 0.0 copy-start.2
  0.0 0.0 copy-start.1
  0.0 41.9 %shard_map.75 = (bf16[8,2,128,128]{3,2,1,0:T(8,128)(2,1)S(1)}, s32[1,1]{1,0:T(1,128)}) custom-call(s32[2,16]{1,0:T(2,128)} %bitcast.22, s32[1,16]{1,0:T(1,128)} %bitcast.28, s32[2,48]{1,0:T(2,128)} %bitcast.24, s32[1,48]{1,0:T(1,128)} %bitcast.30, s32[2,16]{1,0:T(2,128)} %bitcast.26, bf16[32,128,128]{2,1,0:T(8,128)(2,1)} %bitcast.18, ...), custom_call_target="tpu_custom_call" | custom-call | flops 536870912 | bytes 6291456 | tf_op jit(solution)/shard_map/pallas_call | solution.py:311
  42.6 0.0 copy-done.4
  42.6 0.0 copy-done.6
  42.6 0.0 copy-done.3
  42.6 0.0 copy-done
  42.6 0.0 copy-done.5
  42.7 0.0 copy-done.2
  42.7 0.0 copy-done.1
  42.7 0.8 %copy.14 = bf16[1,1,8,2,128,128]{5,4,3,2,1,0:T(8,128)(2,1)} copy(bf16[1,1,8,2,128,128]{5,4,3,2,1,0:T(8,128)(2,1)S(1)} %get-tuple-element.37) | data formatting | bytes 1048576
  (1 shorter events, 0.0 us)
Async XLA Ops:
  0.0 42.6 %copy-start.4 = (s32[1,1,16,2]{2,3,1,0:T(2,128)S(1)}, s32[1,1,16,2]{2,3,1,0:T(2,128)}, u32[]{:S(2)}) copy-start(s32[1,1,16,2]{2,3,1,0:T(2,128)} %param.15) | copy-start | bytes 388
  0.0 42.6 %copy-start.6 = (s32[1,1,1,48]{3,2,1,0:T(1,128)S(1)}, s32[1,1,1,48]{3,2,1,0:T(1,128)}, u32[]{:S(2)}) copy-start(s32[1,1,1,48]{3,2,1,0:T(1,128)} %param.14) | copy-start | bytes 580
  0.0 42.6 %copy-start.3 = (s32[1,1,1,48,2]{3,4,2,1,0:T(2,128)S(1)}, s32[1,1,1,48,2]{3,4,2,1,0:T(2,128)}, u32[]{:S(2)}) copy-start(s32[1,1,1,48,2]{3,4,2,1,0:T(2,128)} %param.13) | copy-start | bytes 1156
  0.0 42.6 %copy-start = (bf16[1,1,1,48,2,128,128]{6,5,4,3,2,1,0:T(8,128)(2,1)S(1)}, bf16[1,1,1,48,2,128,128]{6,5,4,3,2,1,0:T(8,128)(2,1)}, u32[]{:S(2)}) copy-start(bf16[1,1,1,48,2,128,128]{6,5,4,3,2,1,0:T(8,128)(2,1)} %param.12) | copy-start | bytes 9437188
  0.0 42.6 %copy-start.5 = (s32[1,1,1,16]{3,2,1,0:T(1,128)S(1)}, s32[1,1,1,16]{3,2,1,0:T(1,128)}, u32[]{:S(2)}) copy-start(s32[1,1,1,16]{3,2,1,0:T(1,128)} %param.11) | copy-start | bytes 196
  0.0 42.6 %copy-start.2 = (s32[1,1,1,16,2]{3,4,2,1,0:T(2,128)S(1)}, s32[1,1,1,16,2]{3,4,2,1,0:T(2,128)}, u32[]{:S(2)}) copy-start(s32[1,1,1,16,2]{3,4,2,1,0:T(2,128)} %param.10) | copy-start | bytes 388
  0.0 42.6 %copy-start.1 = (bf16[1,1,1,16,2,128,128]{6,5,4,3,2,1,0:T(8,128)(2,1)S(1)}, bf16[1,1,1,16,2,128,128]{6,5,4,3,2,1,0:T(8,128)(2,1)}, u32[]{:S(2)}) copy-start(bf16[1,1,1,16,2,128,128]{6,5,4,3,2,1,0:T(8,128)(2,1)} %param.9) | copy-start | bytes 3145732

commit v4 on v3

--- a/solution.py
+++ b/solution.py
@@ -7,7 +7,8 @@
 from jax.experimental.pallas import tpu as pltpu
 from jax.sharding import PartitionSpec as P
 
-CAPACITY = 32
+SLOTS = 28
+WINDOW = 4
 CHUNKS = 4
 ABSENT = 1000
 LANES = 128
@@ -91,14 +92,14 @@
 
 
 def kernel(
-    n_row, n_col, capacity,
+    n_row, n_col, slots, window, first,
     a_cols_hbm, a_count_hbm, b_cols_hbm, b_count_hbm, c_cols_hbm, a_hbm, b_hbm,
     out_ref, flag_ref,
     a_cols, a_count, b_cols, b_count, c_cols,
     lists_ref, rows_ref,
-    av, bv, a_in, b_first, b_last, packed, part, layer_in, tiles, table_v, table_s, send_v, send_s,
+    av, bv, a_in, b_first, b_last, packed, extra, extra_in, part, layer_in, tiles, table_v, table_s, send_v, send_s,
     flag_own, flag_layer, flag_row_src, flag_row, flag_col_src, flag_col,
-    local_sem, list_send, list_recv, a_send, a_recv, b_send, b_recv, l_send, l_recv,
+    local_sem, list_send, list_recv, a_send, a_recv, b_send, b_recv, e_send, e_recv, l_send, l_recv,
     f0_send, f0_recv, f1_send, f1_recv, f2_send, f2_recv,
 ):
     row = lax.axis_index("row")
@@ -107,6 +108,7 @@
     rows = out_ref.shape[0] * 2
     half = rows // 2
     kb, panel = b_cols.shape
+    capacity = slots + window
 
     def at(d_row, d_col, d_layer=0):
         return {
@@ -114,12 +116,6 @@
             "col": lax.rem(col + d_col + n_col, n_col),
             "layer": lax.rem(layer + d_layer, 2),
         }
-
-    barrier = pltpu.get_barrier_semaphore()
-    partners = [at(o, 0) for o in range(1, n_row)] + [at(0, o) for o in range(1, n_col)]
-    partners += [at(0, 0, 1), at(1, -1), at(-1, 1)]
-    for partner in partners:
-        pl.semaphore_signal(barrier, inc=1, device_id=partner, device_id_type=pl.DeviceIdType.MESH)
 
     loads = [
         pltpu.make_async_copy(src, dst, local_sem.at[4 + k])
@@ -130,18 +126,23 @@
     ]
     for load in loads:
         load.start()
+
+    barrier = pltpu.get_barrier_semaphore()
+    partners = [at(o, 0) for o in range(1, n_row)] + [at(0, o) for o in range(1, n_col)]
+    partners += [at(0, 0, 1), at(1, -1), at(-1, 1)]
+    for partner in partners:
+        pl.semaphore_signal(barrier, inc=1, device_id=partner, device_id_type=pl.DeviceIdType.MESH)
+
+    zero = jnp.zeros(bv.shape[1:], bv.dtype)
+    bv[panel * kb] = zero
+    b_first[first] = zero
+    b_last[capacity - first] = zero
+    for load in loads:
+        load.wait()
     load_b = pltpu.make_async_copy(b_hbm, bv.at[pl.ds(0, panel * kb)], local_sem.at[0])
     load_b.start()
     load_a = pltpu.make_async_copy(a_hbm, av, local_sem.at[1])
     load_a.start()
-    per = capacity // CHUNKS
-    first = capacity - per
-    zero = jnp.zeros(bv.shape[1:], bv.dtype)
-    bv[panel * kb] = zero
-    b_first[first] = zero
-    b_last[per] = zero
-    for load in loads:
-        load.wait()
     fill_lists(lists_ref, rows_ref, a_cols, a_count, b_cols, b_count, c_cols)
     own = lists_ref[...]
     need, place = matched(own[0:1], own[1:2], own[2:], rows, panel, kb)
@@ -162,7 +163,7 @@
         sends[slot] = remote(lists_ref, tiles.at[slot], list_send.at[slot], list_recv.at[slot], device)
     a_copies = []
     a_per = av.shape[0] // CHUNKS
-    for c in range(CHUNKS):
+    for c in (0, CHUNKS // 2, 1, CHUNKS // 2 + 1):
         piece = pl.ds(c * a_per, a_per)
         a_copies.append(
             remote(a_hbm.at[piece], a_in.at[piece], a_send.at[c], a_recv.at[c], at(0, -1))
@@ -179,33 +180,57 @@
     taken = jnp.where(lane == entry, needed * (1 + jnp.broadcast_to(place[0:1], spread)), 0)
     taken = jnp.broadcast_to(jnp.sum(taken, axis=1, keepdims=True), spread)
     here = (jnp.broadcast_to(before, spread) == lane) & (taken > 0)
-    send_v[...] = jnp.sum(jnp.where(here, taken - 1, 0), axis=0, keepdims=True)
+    count = jnp.sum(need, axis=1, keepdims=True)
+    chosen = jnp.sum(jnp.where(here, taken - 1, 0), axis=0, keepdims=True)
+    send_v[...] = jnp.where(lane[0:1] == LANES - 1, count[0:1], chosen)
     to_smem = pltpu.make_async_copy(send_v, send_s, local_sem.at[2])
     to_smem.start()
-    flag_own[...] = jnp.broadcast_to(jnp.sum(need, axis=1, keepdims=True), flag_own.shape)
+    flag_own[...] = jnp.broadcast_to(count, flag_own.shape)
     load_b.wait()
     to_smem.wait()
+    if window:
+        for k in range(window):
+            extra[k] = bv[send_s[0, slots + k]]
+        handed = remote(extra, extra_in, e_send.at[0], e_recv.at[0], at(0, 0, 1))
     b_copies = []
-    for c in range(CHUNKS):
-        for k in range(c * per, (c + 1) * per):
+
+    def send_b(low, high):
+        c = len(b_copies)
+        into, start = (b_first, low) if low < first else (b_last, low - first)
+        landing = into.at[pl.ds(start, high - low)]
+        b_copies.append(
+            remote(packed.at[pl.ds(low, high - low)], landing, b_send.at[c], b_recv.at[c], at(-1, 0))
+        )
+
+    body = slots - window
+    for low, high in ((0, first // 2), (first // 2, first)):
+        for k in range(low, high):
             packed[k] = bv[send_s[0, k]]
-        piece = pl.ds(c * per, per)
-        landing = b_first.at[piece] if c < CHUNKS - 1 else b_last.at[pl.ds(0, per)]
-        b_copies.append(
-            remote(packed.at[piece], landing, b_send.at[c], b_recv.at[c], at(-1, 0))
-        )
+        send_b(low, high)
+    if window:
+        handed.wait_recv()
+        for k in range(body, slots):
+            packed[k] = jnp.where(k < send_s[0, LANES - 1], bv[send_s[0, k]], extra_in[slots - 1 - k])
+        send_b(body, slots)
+    for k in range(first, body):
+        packed[k] = bv[send_s[0, k]]
+    send_b(first, body)
     f0 = remote(flag_own, flag_layer, f0_send.at[0], f0_recv.at[0], at(0, 0, 1))
 
     sends[0].wait_recv()
     sends[1].wait_recv()
     need, place = matched(tiles[0, 0:1], own[1:2], tiles[1][2:], rows, panel, kb)
     before = earlier(need)
-    table_v[1:2] = jnp.where((need > 0) & (before < capacity), before, capacity)[0:1]
+    before = jnp.where((need > 0) & (before < capacity), before, capacity)
+    back = (before >= slots) & (before < capacity)
+    table_v[1:2] = jnp.where(back, slots + capacity - 1 - before, before)[0:1]
     to_smem = pltpu.make_async_copy(table_v, table_s, local_sem.at[3])
     to_smem.start()
 
     f0.wait()
-    flag_row_src[...] = jnp.maximum(flag_own[...], flag_layer[...])
+    crowded = jnp.maximum(flag_own[...], flag_layer[...]) > capacity
+    crowded = crowded | (flag_own[...] + flag_layer[...] > 2 * slots)
+    flag_row_src[...] = jnp.where(crowded, 1, 0)
     f1 = [
         remote(flag_row_src, flag_row.at[o - 1], f1_send.at[o - 1], f1_recv.at[o - 1], at(o, 0))
         for o in range(1, n_row)
@@ -221,7 +246,7 @@
         return b_first[jnp.where(place < first, place, first)]
 
     def from_all(place):
-        last = jnp.where(place < first, per, place - first)
+        last = jnp.where(place < first, capacity - first, place - first)
         return jnp.where(place < first, from_first(place), b_last[last])
 
     def product(a, block, r):
@@ -247,7 +272,7 @@
     for o in range(1, n_col):
         f2[o - 1].wait()
         worst = jnp.maximum(worst, flag_col[o - 1])
-    flag_ref[...] = jnp.where(worst[0:1, 0:1] > capacity, 1, 0)
+    flag_ref[...] = worst[0:1, 0:1]
 
     theirs = (1 - layer) * half
     mine = layer * half
@@ -270,13 +295,23 @@
             )
         )
 
-    for copy in a_copies + b_copies[:-1]:
+    ready = 2 if early <= rows // CHUNKS else CHUNKS
+    for copy in a_copies[:ready] + b_copies[:2]:
         copy.wait_recv()
     add_step(theirs, 0, early, from_first)
     hand_over(0, early)
     add_step(mine, 0, early, from_first)
 
-    b_copies[-1].wait_recv()
+    if window:
+        b_copies[2].wait_recv()
+        back = remote(
+            b_last.at[pl.ds(body - first, window)], b_last.at[pl.ds(slots - first, window)],
+            e_send.at[1], e_recv.at[1], at(0, 0, 1),
+        )
+    for copy in a_copies[ready:] + b_copies[-1:]:
+        copy.wait_recv()
+    if window:
+        back.wait_recv()
     add_step(theirs, early, middle, from_all)
     hand_over(early, middle)
     add_step(theirs, middle, half, from_all)
@@ -292,29 +327,31 @@
             out_ref[k, 0] = total[:, : out_ref.shape[3]]
             out_ref[k, 1] = total[:, out_ref.shape[3] :]
 
-    for copy in list(sends.values()) + a_copies + b_copies + l_copies:
+    shared = [handed, back] if window else []
+    for copy in list(sends.values()) + a_copies + b_copies + shared + l_copies:
         copy.wait_send()
 
 
-def call(n_row, n_col, capacity, collective_id, a_cols, a_count, b_cols, b_count, c_cols, a, b):
+def call(n_row, n_col, slots, window, collective_id, a_cols, a_count, b_cols, b_count, c_cols, a, b):
     ka, rows = a_cols.shape
     kb, panel = b_cols.shape
     kc = c_cols.shape[0]
     size, width = a.shape[1], b.shape[2]
     half = rows // 2
-    per = capacity // CHUNKS
+    capacity = slots + window
+    first = (slots - window) * 2 // 3 // 8 * 8
     vmem = pltpu.VMEM
     dma = pltpu.SemaphoreType.DMA
     tile = (8, LANES)
-    anywhere = pl.BlockSpec(memory_space=pl.ANY)
+    in_hbm = pl.BlockSpec(memory_space=pltpu.HBM)
     in_vmem = pl.BlockSpec(memory_space=vmem)
     return pl.pallas_call(
-        functools.partial(kernel, n_row, n_col, capacity),
+        functools.partial(kernel, n_row, n_col, slots, window, first),
         out_shape=(
             jax.ShapeDtypeStruct((half, kc, size, width), jnp.bfloat16),
             jax.ShapeDtypeStruct((1, 1), jnp.int32),
         ),
-        in_specs=[anywhere] * 7,
+        in_specs=[in_hbm] * 7,
         out_specs=(in_vmem, in_vmem),
         scratch_shapes=[
             vmem(a_cols.shape, jnp.int32),
@@ -327,9 +364,11 @@
             vmem((rows * ka, size, size), jnp.bfloat16),
             vmem((panel * kb + 1, size, width), jnp.bfloat16),
             vmem((rows * ka, size, size), jnp.bfloat16),
-            vmem((capacity - per + 1, size, width), jnp.bfloat16),
-            vmem((per + 1, size, width), jnp.bfloat16),
-            vmem((capacity, size, width), jnp.bfloat16),
+            vmem((first + 1, size, width), jnp.bfloat16),
+            vmem((capacity - first + 1, size, width), jnp.bfloat16),
+            vmem((slots, size, width), jnp.bfloat16),
+            vmem((max(window, 1), size, width), jnp.bfloat16),
+            vmem((max(window, 1), size, width), jnp.bfloat16),
             vmem((rows, size, kc * width), jnp.float32),
             vmem((half, size, kc * width), jnp.float32),
             vmem((4,) + tile, jnp.int32),
@@ -347,13 +386,14 @@
             dma((4,)), dma((4,)),
             dma((CHUNKS,)), dma((CHUNKS,)),
             dma((CHUNKS,)), dma((CHUNKS,)),
+            dma((2,)), dma((2,)),
             dma((3,)), dma((3,)),
             dma((1,)), dma((1,)),
             dma((n_row - 1,)), dma((n_row - 1,)),
             dma((n_col - 1,)), dma((n_col - 1,)),
         ],
         compiler_params=pltpu.CompilerParams(
-            collective_id=collective_id, has_side_effects=True, vmem_limit_bytes=40 * 1024 * 1024
+            collective_id=collective_id, has_side_effects=True, vmem_limit_bytes=62 * 1024 * 1024
         ),
         cost_estimate=pl.CostEstimate(
             flops=4 * rows * size * ka * size * kc * width, bytes_accessed=6 << 20, transcendentals=0
@@ -368,10 +408,10 @@
         a_panel.reshape((-1,) + a_panel.shape[2:]), b_panel.reshape((-1,) + b_panel.shape[2:]),
     )
     every = a_panel.shape[0] * a_panel.shape[1] * c_cols.shape[3]
-    quick, over = call(n_row, n_col, CAPACITY, 0, *args)
+    quick, over = call(n_row, n_col, SLOTS, WINDOW, 0, *args)
     result = lax.cond(
         over[0, 0] > 0,
-        lambda args, quick: call(n_row, n_col, every, 1, *args)[0],
+        lambda args, quick: call(n_row, n_col, every, 0, 1, *args)[0],
         lambda args, quick: quick,
         args, quick,
     )

time: 43.6 us -> 42.4 us (0.972)
  Pallas kernels: 41.9 us -> 40.7 us
    pallas_call x1, Pallas kernels: 41.9 us -> 40.7 us  [call(): pl.pallas_call(functools.partial(kernel, n_row, n_col, slots, window, fir...]
where the time goes in v4:
time: 42.4 us; the launch traced here: 42.3 us
  Pallas kernels  40.7 us (96%)
  local copies, waits for them, and re-layouts  0.82 us (2%)
  between operations  0.7 us (2%)
    pallas_call x1, Pallas kernels, call(): pl.pallas_call(functools.partial(kernel, n_row, n_col, slots, window, fir...  40.7 us

profile of v4, /device:TPU:0, one launch (start us, length us, event | category | flops | bytes accessed | tf_op | source)
XLA Modules:
  0.0 42.3 jit_solution(8755368810574040439)
XLA Ops:
  0.0 0.0 copy-start.3
  0.0 0.0 copy-start.5
  0.0 0.0 copy-start.2
  0.0 0.0 copy-start.4
  0.0 0.0 copy-start.1
  0.0 0.0 copy-start
  0.0 40.7 %shard_map.75 = (bf16[8,2,128,128]{3,2,1,0:T(8,128)(2,1)S(1)}, s32[1,1]{1,0:T(1,128)}) custom-call(s32[2,16]{1,0:T(2,128)} %bitcast.22, s32[1,16]{1,0:T(1,128)} %bitcast.28, s32[2,48]{1,0:T(2,128)} %bitcast.24, s32[1,48]{1,0:T(1,128)} %bitcast.30, s32[2,16]{1,0:T(2,128)} %bitcast.26, bf16[32,128,128]{2,1,0:T(8,128)(2,1)} %bitcast.18, ...), custom_call_target="tpu_custom_call" | custom-call | flops 536870912 | bytes 6291456 | tf_op jit(solution)/shard_map/pallas_call | solution.py:348
  41.4 0.0 copy-done.3
  41.4 0.0 copy-done.5
  41.4 0.0 copy-done.2
  41.4 0.0 copy-done.4
  41.4 0.0 copy-done.1
  41.4 0.0 copy-done
  41.5 0.8 %copy.14 = bf16[1,1,8,2,128,128]{5,4,3,2,1,0:T(8,128)(2,1)} copy(bf16[1,1,8,2,128,128]{5,4,3,2,1,0:T(8,128)(2,1)S(1)} %get-tuple-element.37) | data formatting | bytes 1048576
  (1 shorter events, 0.0 us)
Async XLA Ops:
  0.0 41.4 %copy-start.3 = (s32[1,1,16,2]{2,3,1,0:T(2,128)S(1)}, s32[1,1,16,2]{2,3,1,0:T(2,128)}, u32[]{:S(2)}) copy-start(s32[1,1,16,2]{2,3,1,0:T(2,128)} %param.15) | copy-start | bytes 388
  0.0 41.4 %copy-start.5 = (s32[1,1,1,48]{3,2,1,0:T(1,128)S(1)}, s32[1,1,1,48]{3,2,1,0:T(1,128)}, u32[]{:S(2)}) copy-start(s32[1,1,1,48]{3,2,1,0:T(1,128)} %param.14) | copy-start | bytes 580
  0.0 41.4 %copy-start.2 = (s32[1,1,1,48,2]{3,4,2,1,0:T(2,128)S(1)}, s32[1,1,1,48,2]{3,4,2,1,0:T(2,128)}, u32[]{:S(2)}) copy-start(s32[1,1,1,48,2]{3,4,2,1,0:T(2,128)} %param.13) | copy-start | bytes 1156
  0.0 41.4 %copy-start.4 = (s32[1,1,1,16]{3,2,1,0:T(1,128)S(1)}, s32[1,1,1,16]{3,2,1,0:T(1,128)}, u32[]{:S(2)}) copy-start(s32[1,1,1,16]{3,2,1,0:T(1,128)} %param.11) | copy-start | bytes 196
  0.0 41.4 %copy-start.1 = (s32[1,1,1,16,2]{3,4,2,1,0:T(2,128)S(1)}, s32[1,1,1,16,2]{3,4,2,1,0:T(2,128)}, u32[]{:S(2)}) copy-start(s32[1,1,1,16,2]{3,4,2,1,0:T(2,128)} %param.10) | copy-start | bytes 388
  0.0 41.4 %copy-start = (bf16[1,1,1,16,2,128,128]{6,5,4,3,2,1,0:T(8,128)(2,1)S(1)}, bf16[1,1,1,16,2,128,128]{6,5,4,3,2,1,0:T(8,128)(2,1)}, u32[]{:S(2)}) copy-start(bf16[1,1,1,16,2,128,128]{6,5,4,3,2,1,0:T(8,128)(2,1)} %param.9) | copy-start | bytes 3145732

commit v5 on v4

--- a/solution.py
+++ b/solution.py
@@ -97,7 +97,7 @@
     out_ref, flag_ref,
     a_cols, a_count, b_cols, b_count, c_cols,
     lists_ref, rows_ref,
-    av, bv, a_in, b_first, b_last, packed, extra, extra_in, part, layer_in, tiles, table_v, table_s, send_v, send_s,
+    av, bv, a_in, b_first, b_all, packed, extra, extra_in, part, layer_in, tiles, table_v, table_s, send_v, send_s,
     flag_own, flag_layer, flag_row_src, flag_row, flag_col_src, flag_col,
     local_sem, list_send, list_recv, a_send, a_recv, b_send, b_recv, e_send, e_recv, l_send, l_recv,
     f0_send, f0_recv, f1_send, f1_recv, f2_send, f2_recv,
@@ -136,7 +136,7 @@
     zero = jnp.zeros(bv.shape[1:], bv.dtype)
     bv[panel * kb] = zero
     b_first[first] = zero
-    b_last[capacity - first] = zero
+    b_all[capacity] = zero
     for load in loads:
         load.wait()
     load_b = pltpu.make_async_copy(b_hbm, bv.at[pl.ds(0, panel * kb)], local_sem.at[0])
@@ -186,6 +186,7 @@
     to_smem = pltpu.make_async_copy(send_v, send_s, local_sem.at[2])
     to_smem.start()
     flag_own[...] = jnp.broadcast_to(count, flag_own.shape)
+    f0 = remote(flag_own, flag_layer, f0_send.at[0], f0_recv.at[0], at(0, 0, 1))
     load_b.wait()
     to_smem.wait()
     if window:
@@ -196,8 +197,7 @@
 
     def send_b(low, high):
         c = len(b_copies)
-        into, start = (b_first, low) if low < first else (b_last, low - first)
-        landing = into.at[pl.ds(start, high - low)]
+        landing = (b_first if low < first else b_all).at[pl.ds(low, high - low)]
         b_copies.append(
             remote(packed.at[pl.ds(low, high - low)], landing, b_send.at[c], b_recv.at[c], at(-1, 0))
         )
@@ -207,6 +207,14 @@
         for k in range(low, high):
             packed[k] = bv[send_s[0, k]]
         send_b(low, high)
+    f0.wait()
+    crowded = jnp.maximum(flag_own[...], flag_layer[...]) > capacity
+    crowded = crowded | (flag_own[...] + flag_layer[...] > 2 * slots)
+    flag_row_src[...] = jnp.where(crowded, 1, 0)
+    f1 = [
+        remote(flag_row_src, flag_row.at[o - 1], f1_send.at[o - 1], f1_recv.at[o - 1], at(o, 0))
+        for o in range(1, n_row)
+    ]
     if window:
         handed.wait_recv()
         for k in range(body, slots):
@@ -215,7 +223,6 @@
     for k in range(first, body):
         packed[k] = bv[send_s[0, k]]
     send_b(first, body)
-    f0 = remote(flag_own, flag_layer, f0_send.at[0], f0_recv.at[0], at(0, 0, 1))
 
     sends[0].wait_recv()
     sends[1].wait_recv()
@@ -227,14 +234,6 @@
     to_smem = pltpu.make_async_copy(table_v, table_s, local_sem.at[3])
     to_smem.start()
 
-    f0.wait()
-    crowded = jnp.maximum(flag_own[...], flag_layer[...]) > capacity
-    crowded = crowded | (flag_own[...] + flag_layer[...] > 2 * slots)
-    flag_row_src[...] = jnp.where(crowded, 1, 0)
-    f1 = [
-        remote(flag_row_src, flag_row.at[o - 1], f1_send.at[o - 1], f1_recv.at[o - 1], at(o, 0))
-        for o in range(1, n_row)
-    ]
     to_smem.wait()
     load_a.wait()
 
@@ -244,10 +243,6 @@
 
     def from_first(place):
         return b_first[jnp.where(place < first, place, first)]
-
-    def from_all(place):
-        last = jnp.where(place < first, capacity - first, place - first)
-        return jnp.where(place < first, from_first(place), b_last[last])
 
     def product(a, block, r):
         left = jnp.concatenate([a[2 * r], a[2 * r + 1]], axis=1)
@@ -259,6 +254,43 @@
     @pl.loop(0, rows, unroll=4)
     def _(r):
         part[r] = product(av, [bv[place] for place in blocks_of(0, r)], r)
+
+    theirs = (1 - layer) * half
+    mine = layer * half
+    early = first // 8
+    middle = (early + half + 1) // 2
+    l_copies = []
+
+    def step_one(read, r):
+        return part[r] + product(a_in, [read(place) for place in blocks_of(1, r)], r)
+
+    def for_other(low, high, read):
+        @pl.loop(low, high, unroll=high - low)
+        def _(k):
+            part[theirs + k] = step_one(read, theirs + k)
+
+        hand_over(low, high)
+
+    def for_result(low, high, read):
+        @pl.loop(low, high, unroll=high - low)
+        def _(k):
+            total = (step_one(read, mine + k) + layer_in[k]).astype(out_ref.dtype)
+            out_ref[k, 0] = total[:, : out_ref.shape[3]]
+            out_ref[k, 1] = total[:, out_ref.shape[3] :]
+
+    def hand_over(low, high):
+        c = len(l_copies)
+        l_copies.append(
+            remote(
+                part.at[pl.ds(theirs + low, high - low)], layer_in.at[pl.ds(low, high - low)],
+                l_send.at[c], l_recv.at[c], at(0, 0, 1),
+            )
+        )
+
+    ready = 2 if early <= rows // CHUNKS else CHUNKS
+    for copy in a_copies[:ready] + b_copies[:2]:
+        copy.wait_recv()
+    for_other(0, early, from_first)
 
     worst = flag_row_src[...]
     for o in range(1, n_row):
@@ -269,63 +301,39 @@
         remote(flag_col_src, flag_col.at[o - 1], f2_send.at[o - 1], f2_recv.at[o - 1], at(0, o))
         for o in range(1, n_col)
     ]
+
+    @pl.loop(0, first, unroll=4)
+    def _(k):
+        b_all[k] = b_first[k]
+
+    l_copies[0].wait_recv()
+    for_result(0, early, from_first)
+
+    if window:
+        b_copies[2].wait_recv()
+        back = remote(
+            b_all.at[pl.ds(body, window)], b_all.at[pl.ds(slots, window)],
+            e_send.at[1], e_recv.at[1], at(0, 0, 1),
+        )
+    for copy in a_copies[ready:] + b_copies[-1:]:
+        copy.wait_recv()
+    if window:
+        back.wait_recv()
+
+    def from_all(place):
+        return b_all[place]
+
+    for_other(early, middle, from_all)
+    for_other(middle, half, from_all)
+    l_copies[1].wait_recv()
+    for_result(early, middle, from_all)
+    l_copies[2].wait_recv()
+    for_result(middle, half, from_all)
+
     for o in range(1, n_col):
         f2[o - 1].wait()
         worst = jnp.maximum(worst, flag_col[o - 1])
     flag_ref[...] = worst[0:1, 0:1]
-
-    theirs = (1 - layer) * half
-    mine = layer * half
-    early = first // 8
-    middle = (early + half + 1) // 2
-    l_copies = []
-
-    def add_step(base, low, high, read):
-        @pl.loop(low, high, unroll=high - low)
-        def _(k):
-            r = base + k
-            part[r] += product(a_in, [read(place) for place in blocks_of(1, r)], r)
-
-    def hand_over(low, high):
-        c = len(l_copies)
-        l_copies.append(
-            remote(
-                part.at[pl.ds(theirs + low, high - low)], layer_in.at[pl.ds(low, high - low)],
-                l_send.at[c], l_recv.at[c], at(0, 0, 1),
-            )
-        )
-
-    ready = 2 if early <= rows // CHUNKS else CHUNKS
-    for copy in a_copies[:ready] + b_copies[:2]:
-        copy.wait_recv()
-    add_step(theirs, 0, early, from_first)
-    hand_over(0, early)
-    add_step(mine, 0, early, from_first)
-
-    if window:
-        b_copies[2].wait_recv()
-        back = remote(
-            b_last.at[pl.ds(body - first, window)], b_last.at[pl.ds(slots - first, window)],
-            e_send.at[1], e_recv.at[1], at(0, 0, 1),
-        )
-    for copy in a_copies[ready:] + b_copies[-1:]:
-        copy.wait_recv()
-    if window:
-        back.wait_recv()
-    add_step(theirs, early, middle, from_all)
-    hand_over(early, middle)
-    add_step(theirs, middle, half, from_all)
-    hand_over(middle, half)
-    add_step(mine, early, half, from_all)
-
-    for copy, (low, high) in zip(l_copies, ((0, early), (early, middle), (middle, half))):
-        copy.wait_recv()
-
-        @pl.loop(low, high, unroll=high - low)
-        def _(k):
-            total = (part[mine + k] + layer_in[k]).astype(out_ref.dtype)
-            out_ref[k, 0] = total[:, : out_ref.shape[3]]
-            out_ref[k, 1] = total[:, out_ref.shape[3] :]
 
     shared = [handed, back] if window else []
     for copy in list(sends.values()) + a_copies + b_copies + shared + l_copies:
@@ -365,7 +373,7 @@
             vmem((panel * kb + 1, size, width), jnp.bfloat16),
             vmem((rows * ka, size, size), jnp.bfloat16),
             vmem((first + 1, size, width), jnp.bfloat16),
-            vmem((capacity - first + 1, size, width), jnp.bfloat16),
+            vmem((capacity + 1, size, width), jnp.bfloat16),
             vmem((slots, size, width), jnp.bfloat16),
             vmem((max(window, 1), size, width), jnp.bfloat16),
             vmem((max(window, 1), size, width), jnp.bfloat16),

time: 42.4 us -> 35.3 us (0.83); the launches traced: 42.3 us -> 34.7 us
  Pallas kernels: 40.7 us -> 33.1 us
    pallas_call x1, Pallas kernels: 40.7 us -> 33.1 us  [call(): pl.pallas_call(functools.partial(kernel, n_row, n_col, slots, window, fir...]
where the time goes in v5:
time: 35.3 us; the launch traced here: 34.7 us
  Pallas kernels  33.1 us (94%)
  local copies, waits for them, and re-layouts  0.82 us (2%)
  between operations  0.7 us (2%)
    pallas_call x1, Pallas kernels, call(): pl.pallas_call(functools.partial(kernel, n_row, n_col, slots, window, fir...  33.1 us
    unnamed x13, local copies, waits for them, and re-layouts  0.82 us

profile of v5, /device:TPU:0, one launch (start us, length us, event | category | flops | bytes accessed | tf_op | source)
XLA Modules:
  0.0 34.7 jit_solution(15613871606885530496)
XLA Ops:
  0.0 0.0 copy-start.3
  0.0 0.0 copy-start.5
  0.0 0.0 copy-start.2
  0.0 0.0 copy-start.4
  0.0 0.0 copy-start.1
  0.0 0.0 copy-start
  0.0 33.1 %shard_map.75 = (bf16[8,2,128,128]{3,2,1,0:T(8,128)(2,1)S(1)}, s32[1,1]{1,0:T(1,128)}) custom-call(s32[2,16]{1,0:T(2,128)} %bitcast.22, s32[1,16]{1,0:T(1,128)} %bitcast.28, s32[2,48]{1,0:T(2,128)} %bitcast.24, s32[1,48]{1,0:T(1,128)} %bitcast.30, s32[2,16]{1,0:T(2,128)} %bitcast.26, bf16[32,128,128]{2,1,0:T(8,128)(2,1)} %bitcast.18, ...), custom_call_target="tpu_custom_call" | custom-call | flops 536870912 | bytes 6291456 | tf_op jit(solution)/shard_map/pallas_call | solution.py:356
  33.8 0.0 copy-done.3
  33.8 0.0 copy-done.5
  33.8 0.0 copy-done.2
  33.8 0.0 copy-done.4
  33.8 0.0 copy-done.1
  33.8 0.0 copy-done
  33.9 0.8 %copy.14 = bf16[1,1,8,2,128,128]{5,4,3,2,1,0:T(8,128)(2,1)} copy(bf16[1,1,8,2,128,128]{5,4,3,2,1,0:T(8,128)(2,1)S(1)} %get-tuple-element.37) | data formatting | bytes 1048576
  (1 shorter events, 0.0 us)
Async XLA Ops:
  0.0 33.8 %copy-start.3 = (s32[1,1,16,2]{2,3,1,0:T(2,128)S(1)}, s32[1,1,16,2]{2,3,1,0:T(2,128)}, u32[]{:S(2)}) copy-start(s32[1,1,16,2]{2,3,1,0:T(2,128)} %param.15) | copy-start | bytes 388
  0.0 33.8 %copy-start.5 = (s32[1,1,1,48]{3,2,1,0:T(1,128)S(1)}, s32[1,1,1,48]{3,2,1,0:T(1,128)}, u32[]{:S(2)}) copy-start(s32[1,1,1,48]{3,2,1,0:T(1,128)} %param.14) | copy-start | bytes 580
  0.0 33.8 %copy-start.2 = (s32[1,1,1,48,2]{3,4,2,1,0:T(2,128)S(1)}, s32[1,1,1,48,2]{3,4,2,1,0:T(2,128)}, u32[]{:S(2)}) copy-start(s32[1,1,1,48,2]{3,4,2,1,0:T(2,128)} %param.13) | copy-start | bytes 1156
  0.0 33.8 %copy-start.4 = (s32[1,1,1,16]{3,2,1,0:T(1,128)S(1)}, s32[1,1,1,16]{3,2,1,0:T(1,128)}, u32[]{:S(2)}) copy-start(s32[1,1,1,16]{3,2,1,0:T(1,128)} %param.11) | copy-start | bytes 196
  0.0 33.8 %copy-start.1 = (s32[1,1,1,16,2]{3,4,2,1,0:T(2,128)S(1)}, s32[1,1,1,16,2]{3,4,2,1,0:T(2,128)}, u32[]{:S(2)}) copy-start(s32[1,1,1,16,2]{3,4,2,1,0:T(2,128)} %param.10) | copy-start | bytes 388
  0.0 33.8 %copy-start = (bf16[1,1,1,16,2,128,128]{6,5,4,3,2,1,0:T(8,128)(2,1)S(1)}, bf16[1,1,1,16,2,128,128]{6,5,4,3,2,1,0:T(8,128)(2,1)}, u32[]{:S(2)}) copy-start(bf16[1,1,1,16,2,128,128]{6,5,4,3,2,1,0:T(8,128)(2,1)} %param.9) | copy-start | bytes 3145732

commit v6 on v5

--- a/solution.py
+++ b/solution.py
@@ -9,6 +9,8 @@
 
 SLOTS = 28
 WINDOW = 4
+FIRST = 20
+EARLY = 4
 CHUNKS = 4
 ABSENT = 1000
 LANES = 128
@@ -92,7 +94,7 @@
 
 
 def kernel(
-    n_row, n_col, slots, window, first,
+    n_row, n_col, slots, window, first, early,
     a_cols_hbm, a_count_hbm, b_cols_hbm, b_count_hbm, c_cols_hbm, a_hbm, b_hbm,
     out_ref, flag_ref,
     a_cols, a_count, b_cols, b_count, c_cols,
@@ -185,7 +187,9 @@
     send_v[...] = jnp.where(lane[0:1] == LANES - 1, count[0:1], chosen)
     to_smem = pltpu.make_async_copy(send_v, send_s, local_sem.at[2])
     to_smem.start()
-    flag_own[...] = jnp.broadcast_to(count, flag_own.shape)
+    soon = jnp.where(lax.broadcasted_iota(jnp.int32, need.shape, 1) < 8 * early, need, 0)
+    soon = jnp.sum(soon, axis=1, keepdims=True)
+    flag_own[...] = jnp.broadcast_to(jnp.where(soon > first, ABSENT, count), flag_own.shape)
     f0 = remote(flag_own, flag_layer, f0_send.at[0], f0_recv.at[0], at(0, 0, 1))
     load_b.wait()
     to_smem.wait()
@@ -257,7 +261,6 @@
 
     theirs = (1 - layer) * half
     mine = layer * half
-    early = first // 8
     middle = (early + half + 1) // 2
     l_copies = []
 
@@ -340,21 +343,20 @@
         copy.wait_send()
 
 
-def call(n_row, n_col, slots, window, collective_id, a_cols, a_count, b_cols, b_count, c_cols, a, b):
+def call(n_row, n_col, slots, window, first, early, collective_id, a_cols, a_count, b_cols, b_count, c_cols, a, b):
     ka, rows = a_cols.shape
     kb, panel = b_cols.shape
     kc = c_cols.shape[0]
     size, width = a.shape[1], b.shape[2]
     half = rows // 2
     capacity = slots + window
-    first = (slots - window) * 2 // 3 // 8 * 8
     vmem = pltpu.VMEM
     dma = pltpu.SemaphoreType.DMA
     tile = (8, LANES)
     in_hbm = pl.BlockSpec(memory_space=pltpu.HBM)
     in_vmem = pl.BlockSpec(memory_space=vmem)
     return pl.pallas_call(
-        functools.partial(kernel, n_row, n_col, slots, window, first),
+        functools.partial(kernel, n_row, n_col, slots, window, first, early),
         out_shape=(
             jax.ShapeDtypeStruct((half, kc, size, width), jnp.bfloat16),
             jax.ShapeDtypeStruct((1, 1), jnp.int32),
@@ -416,10 +418,10 @@
         a_panel.reshape((-1,) + a_panel.shape[2:]), b_panel.reshape((-1,) + b_panel.shape[2:]),
     )
     every = a_panel.shape[0] * a_panel.shape[1] * c_cols.shape[3]
-    quick, over = call(n_row, n_col, SLOTS, WINDOW, 0, *args)
+    quick, over = call(n_row, n_col, SLOTS, WINDOW, FIRST, EARLY, 0, *args)
     result = lax.cond(
         over[0, 0] > 0,
-        lambda args, quick: call(n_row, n_col, every, 0, 1, *args)[0],
+        lambda args, quick: call(n_row, n_col, every, 0, every // 2, every // 16, 1, *args)[0],
         lambda args, quick: quick,
         args, quick,
     )

time: 35.3 us -> 34.9 us (0.989); the launches traced: 34.7 us -> 34.7 us
  no operation moved by 1% of the time
where the time goes in v6:
time: 34.9 us; the launch traced here: 34.7 us
  Pallas kernels  33.2 us (95%)
  local copies, waits for them, and re-layouts  0.82 us (2%)
  between operations  0.7 us (2%)
    pallas_call x1, Pallas kernels, call(): pl.pallas_call(functools.partial(kernel, n_row, n_col, slots, window, fir...  33.2 us
    unnamed x13, local copies, waits for them, and re-layouts  0.82 us

profile of v6, /device:TPU:0, one launch (start us, length us, event | category | flops | bytes accessed | tf_op | source)
XLA Modules:
  0.0 34.7 jit_solution(15228301803938815658)
XLA Ops:
  0.0 0.0 copy-start.3
  0.0 0.0 copy-start.5
  0.0 0.0 copy-start.2
  0.0 0.0 copy-start.4
  0.0 0.0 copy-start.1
  0.0 0.0 copy-start
  0.0 33.2 %shard_map.75 = (bf16[8,2,128,128]{3,2,1,0:T(8,128)(2,1)S(1)}, s32[1,1]{1,0:T(1,128)}) custom-call(s32[2,16]{1,0:T(2,128)} %bitcast.22, s32[1,16]{1,0:T(1,128)} %bitcast.28, s32[2,48]{1,0:T(2,128)} %bitcast.24, s32[1,48]{1,0:T(1,128)} %bitcast.30, s32[2,16]{1,0:T(2,128)} %bitcast.26, bf16[32,128,128]{2,1,0:T(8,128)(2,1)} %bitcast.18, ...), custom_call_target="tpu_custom_call" | custom-call | flops 536870912 | bytes 6291456 | tf_op jit(solution)/shard_map/pallas_call | solution.py:358
  33.8 0.0 copy-done.3
  33.8 0.0 copy-done.5
  33.8 0.0 copy-done.2
  33.8 0.0 copy-done.4
  33.9 0.0 copy-done.1
  33.9 0.0 copy-done
  33.9 0.8 %copy.14 = bf16[1,1,8,2,128,128]{5,4,3,2,1,0:T(8,128)(2,1)} copy(bf16[1,1,8,2,128,128]{5,4,3,2,1,0:T(8,128)(2,1)S(1)} %get-tuple-element.37) | data formatting | bytes 1048576
  (1 shorter events, 0.0 us)
Async XLA Ops:
  0.0 33.8 %copy-start.3 = (s32[1,1,16,2]{2,3,1,0:T(2,128)S(1)}, s32[1,1,16,2]{2,3,1,0:T(2,128)}, u32[]{:S(2)}) copy-start(s32[1,1,16,2]{2,3,1,0:T(2,128)} %param.15) | copy-start | bytes 388
  0.0 33.8 %copy-start.5 = (s32[1,1,1,48]{3,2,1,0:T(1,128)S(1)}, s32[1,1,1,48]{3,2,1,0:T(1,128)}, u32[]{:S(2)}) copy-start(s32[1,1,1,48]{3,2,1,0:T(1,128)} %param.14) | copy-start | bytes 580
  0.0 33.8 %copy-start.2 = (s32[1,1,1,48,2]{3,4,2,1,0:T(2,128)S(1)}, s32[1,1,1,48,2]{3,4,2,1,0:T(2,128)}, u32[]{:S(2)}) copy-start(s32[1,1,1,48,2]{3,4,2,1,0:T(2,128)} %param.13) | copy-start | bytes 1156
  0.0 33.8 %copy-start.4 = (s32[1,1,1,16]{3,2,1,0:T(1,128)S(1)}, s32[1,1,1,16]{3,2,1,0:T(1,128)}, u32[]{:S(2)}) copy-start(s32[1,1,1,16]{3,2,1,0:T(1,128)} %param.11) | copy-start | bytes 196
  0.0 33.8 %copy-start.1 = (s32[1,1,1,16,2]{3,4,2,1,0:T(2,128)S(1)}, s32[1,1,1,16,2]{3,4,2,1,0:T(2,128)}, u32[]{:S(2)}) copy-start(s32[1,1,1,16,2]{3,4,2,1,0:T(2,128)} %param.10) | copy-start | bytes 388
  0.0 33.9 %copy-start = (bf16[1,1,1,16,2,128,128]{6,5,4,3,2,1,0:T(8,128)(2,1)S(1)}, bf16[1,1,1,16,2,128,128]{6,5,4,3,2,1,0:T(8,128)(2,1)}, u32[]{:S(2)}) copy-start(bf16[1,1,1,16,2,128,128]{6,5,4,3,2,1,0:T(8,128)(2,1)} %param.9) | copy-start | bytes 3145732
